TPU v7x, 256 devices: a whole 4x4x8 slice. The times are simulated.
256 devices in a mesh: ctx: 128 (over y_lo, x, z, core), head: 2 (over y_hi).
Axes of the slice: x: 4, y: 4 (y_hi: 2, y_lo: 2; y = y_hi * 2 + y_lo), z: 8, core: 2. Of those that a mesh axis runs over, the one named last changes fastest.
Arguments:
- queries: bfloat16 [32768, 4096], P(('ctx', 'head')), may hold values from -150 to 150
- keys: bfloat16 [32768, 1024], P(('ctx', 'head')), may hold values from -6 to 6
- values: bfloat16 [32768, 1024], P(('ctx', 'head')), may hold values from -6 to 6
- block_place: int32 [256], replicated, may hold values from 0 to 255, each once
Outputs:
- attention: bfloat16 [32768, 4096], P(('ctx', 'head'))
Inputs may be any that keep to these rules, and one draw needn't show every extreme that they name: `block_place`: each of 0 to 255 appears once.
All inputs are finite; a program needn't handle non-finite values.
Results may differ from a plain program's by a relative error of at most 0.0037.
Values may be sent and summed in bfloat16 or wider, within the bound.
No kernel may reach another device: no remote copies, remote signals or barrier semaphores. Data moves between devices by JAX's collectives and lax.ppermute only.
A program may use at most 128 MiB of HBM per device.

v0:
```python
import jax
import jax.numpy as jnp
from jax import lax
from jax.sharding import PartitionSpec as P

HEAD_DIM = 128
WINDOW_STEPS = 3


NEGATIVE = -1e30


def from_behind(array, axis, by):
    devices = lax.axis_size(axis)
    return lax.ppermute(array, axis, [(i, (i + by) % devices) for i in range(devices)])


def tile_part(q_half, k_half, v_half, q_place, k_place):
    rows = q_half.shape[0]
    groups = k_half.shape[1] // HEAD_DIM
    share = q_half.shape[1] // k_half.shape[1]
    q_four = q_half.reshape(rows, groups, share, HEAD_DIM)
    k_three = k_half.reshape(rows, groups, HEAD_DIM)
    v_three = v_half.reshape(rows, groups, HEAD_DIM)
    scores = jnp.einsum(
        "agrd,bgd->grab", q_four, k_three, preferred_element_type=jnp.float32
    ) * HEAD_DIM ** (-0.5)
    offsets = jnp.arange(rows, dtype=jnp.int32)
    visible = (k_place * rows + offsets)[None, :] <= (q_place * rows + offsets)[:, None]
    peak = jnp.max(jnp.where(visible, scores, NEGATIVE), axis=-1)
    weights = jnp.exp(jnp.where(visible, scores - peak[..., None], NEGATIVE))
    total = jnp.sum(weights, axis=-1)
    rounded = weights.astype(jnp.bfloat16)
    output = jnp.einsum("grab,bgd->agrd", rounded, v_three, preferred_element_type=jnp.float32)
    return (output.reshape(rows, -1), peak.reshape(-1, rows), total.reshape(-1, rows))


def visit(operands):
    return tile_part(*operands)


def combine(first, second):
    out_a, peak_a, sum_a = first
    out_b, peak_b, sum_b = second
    peak = jnp.maximum(peak_a, peak_b)
    scale_a = jnp.exp(peak_a - peak)
    scale_b = jnp.exp(peak_b - peak)
    rows = out_a.shape[0]
    heads = peak.shape[0]
    mixed = (
        out_a.reshape(rows, heads, -1) * scale_a.T[:, :, None]
        + out_b.reshape(rows, heads, -1) * scale_b.T[:, :, None]
    )
    return (mixed.reshape(rows, -1), peak, sum_a * scale_a + sum_b * scale_b)


def block_part(q_block, q_pair, k_block, v_block, k_pair):
    half = q_block.shape[0] // 2
    results = []
    for first in range(2):
        merged = None
        for second in range(2):
            operands = (
                q_block[first * half : (first + 1) * half],
                k_block[second * half : (second + 1) * half],
                v_block[second * half : (second + 1) * half],
                q_pair[first],
                k_pair[second],
            )
            part = visit(operands)
            merged = part if merged is None else combine(merged, part)
        results.append(merged)
    return (
        jnp.concatenate([results[0][0], results[1][0]], axis=0),
        jnp.concatenate([results[0][1], results[1][1]], axis=1),
        jnp.concatenate([results[0][2], results[1][2]], axis=1),
    )


def shards(queries, keys, values, block_place):
    q_block, k_block, v_block = (
        lax.all_to_all(queries, "head", split_axis=1, concat_axis=0, tiled=True),
        lax.all_to_all(keys, "head", split_axis=1, concat_axis=0, tiled=True),
        lax.all_to_all(values, "head", split_axis=1, concat_axis=0, tiled=True),
    )
    cycle = lax.axis_size("ctx")
    own_index = lax.axis_index("ctx")

    def pair_of(index):
        return lax.dynamic_slice(block_place, (2 * (index % cycle),), (2,))

    own_pair = pair_of(own_index)
    gathered = block_part(q_block, own_pair, k_block, v_block, own_pair)
    moving = q_block
    parts = []
    for step in range(1, WINDOW_STEPS + 1):
        moving = from_behind(moving, "ctx", 1)
        parts.append(block_part(moving, pair_of(own_index - step), k_block, v_block, own_pair))
    for step in range(1, WINDOW_STEPS + 1):
        piece = parts[step - 1]
        gathered = combine(gathered, from_behind((piece[0], piece[1], piece[2]), "ctx", -step))
    out_block, peak, denom = gathered
    rows = out_block.shape[0]
    heads = peak.shape[0]
    attention = (
        (out_block.reshape(rows, heads, -1) / denom.T[:, :, None])
        .reshape(rows, -1)
        .astype(jnp.bfloat16)
    )
    return lax.all_to_all(attention, "head", split_axis=0, concat_axis=1, tiled=True)


def solution(mesh):
    in_specs = (P(("ctx", "head"), None), P(("ctx", "head"), None), P(("ctx", "head"), None), P())
    out_specs = P(("ctx", "head"), None)
    return jax.shard_map(shards, mesh=mesh, in_specs=in_specs, out_specs=out_specs, check_vma=False)
```

profile of v0, /device:TPU:239, one launch (start us, length us, event | category | flops | bytes accessed | tf_op | source)
XLA Modules:
  0.0 250.7 jit_solution(14682075199457929762)
XLA Ops:
  0.0 1.9 copy.141
  1.9 3.4 %all-to-all-start = ((bf16[128,2,512]{0,2,1:T(8,128)(2,1)}), bf16[128,2,512]{0,2,1:T(8,128)(2,1)S(1)}, u32[]{:S(2)}, u32[]{:S(2)}) async-start(bf16[128,2,512]{0,2,1:T(8,128)(2,1)} %bitcast.1), calls=%async_computation | async-start | bytes 524288 | tf_op jit(solution)/shard_map/all_to_all | solution.py:83
  5.4 0.9 fusion.196
  6.3 0.6 fusion.197
  9.5 0.7 fusion.199
  12.0 1.8 copy.254
  13.8 4.1 %all-to-all-start.2 = ((bf16[128,2,512]{0,2,1:T(8,128)(2,1)}), bf16[128,2,512]{0,2,1:T(8,128)(2,1)S(1)}, u32[]{:S(2)}, u32[]{:S(2)}) async-start(bf16[128,2,512]{0,2,1:T(8,128)(2,1)} %bitcast.9), calls=%async_computation.2 | async-start | bytes 524288 | tf_op jit(solution)/shard_map/all_to_all | solution.py:84
  18.6 1.3 copy.142
  19.9 3.6 %all-to-all-done.2 = bf16[128,2,512]{0,2,1:T(8,128)(2,1)S(1)} async-done(((bf16[128,2,512]{0,2,1:T(8,128)(2,1)}), bf16[128,2,512]{0,2,1:T(8,128)(2,1)S(1)}, u32[]{:S(2)}, u32[]{:S(2)}) %all-to-all-start.2) | async-done | bytes 262176 | tf_op jit(solution)/shard_map/all_to_all | solution.py:84
  23.5 3.6 %all-to-all-start.1 = ((bf16[128,2,2048]{0,2,1:T(8,128)(2,1)}), bf16[128,2,2048]{0,2,1:T(8,128)(2,1)S(1)}, u32[]{:S(2)}, u32[]{:S(2)}) async-start(bf16[128,2,2048]{0,2,1:T(8,128)(2,1)} %bitcast.5), calls=%async_computation.1 | async-start | bytes 2097152 | tf_op jit(solution)/shard_map/all_to_all | solution.py:82
  27.4 12.3 %all-to-all-done.1 = bf16[128,2,2048]{0,2,1:T(8,128)(2,1)S(1)} async-done(((bf16[128,2,2048]{0,2,1:T(8,128)(2,1)}), bf16[128,2,2048]{0,2,1:T(8,128)(2,1)S(1)}, u32[]{:S(2)}, u32[]{:S(2)}) %all-to-all-start.1) | async-done | bytes 1048608 | tf_op jit(solution)/shard_map/all_to_all | solution.py:82
  39.7 1.3 copy.156
  41.0 0.4 select_reduce_fusion.12
  42.0 0.4 select_reduce_fusion.13
  42.9 1.0 collective-permute-start
  44.0 1.2 fusion.29
  45.2 0.4 select_reduce_fusion.14
  45.7 0.4 select_reduce_fusion.15
  46.3 9.7 %collective-permute-done = bf16[256,2048]{1,0:T(8,128)(2,1)S(1)} collective-permute-done((bf16[256,2048]{1,0:T(8,128)(2,1)}, bf16[256,2048]{1,0:T(8,128)(2,1)S(1)}, u32[]{:S(2)}, u32[]{:S(2)}) %collective-permute-start) | collective-permute-done | bytes 1048608 | tf_op jit(solution)/shard_map/ppermute | solution.py:15
  56.0 1.2 fusion.191
  57.3 1.3 copy.162
  58.6 0.4 select_reduce_fusion.8
  59.2 1.3 fusion.79
  60.5 0.4 select_reduce_fusion.9
  61.1 1.4 fusion.81
  62.5 1.3 copy.157
  63.8 0.4 select_reduce_fusion.10
  64.2 0.4 select_reduce_fusion.11
  65.0 0.4 copy-done.3
  66.2 6.6 %collective-permute-start.3 = (bf16[256,2048]{1,0:T(8,128)(2,1)S(1)}, bf16[256,2048]{1,0:T(8,128)(2,1)S(1)}, u32[]{:S(2)}, u32[]{:S(2)}) collective-permute-start(bf16[256,2048]{1,0:T(8,128)(2,1)S(1)} %copy-done.9), channel_id=1, source_target_pairs={{0,2},{2,4},{4,6},{6,8},{8,10},{10,12},{12,14},{14,16},{16,18},{18... | collective-permute-start | bytes 3145736 | tf_op jit(solution)/shard_map/ppermute | solution.py:15
  73.6 1.4 pad_maximum_fusion
  75.1 9.5 %collective-permute-done.3 = bf16[256,2048]{1,0:T(8,128)(2,1)S(1)} collective-permute-done((bf16[256,2048]{1,0:T(8,128)(2,1)S(1)}, bf16[256,2048]{1,0:T(8,128)(2,1)S(1)}, u32[]{:S(2)}, u32[]{:S(2)}) %collective-permute-start.3) | collective-permute-done | bytes 1048608 | tf_op jit(solution)/shard_map/ppermute | solution.py:15
  84.6 1.2 fusion.192
  85.9 1.3 copy.176
  87.2 0.4 select_reduce_fusion.4
  87.8 1.3 fusion.71
  89.1 0.4 select_reduce_fusion.5
  89.7 1.4 fusion.73
  91.0 1.3 copy.171
  92.4 0.4 select_reduce_fusion.6
  92.8 0.4 select_reduce_fusion.7
  93.6 0.4 copy-done.4
  94.8 6.7 %collective-permute-start.6 = (bf16[256,2048]{1,0:T(8,128)(2,1)S(1)}, bf16[256,2048]{1,0:T(8,128)(2,1)S(1)}, u32[]{:S(2)}, u32[]{:S(2)}) collective-permute-start(bf16[256,2048]{1,0:T(8,128)(2,1)S(1)} %copy-done.11), channel_id=1, source_target_pairs={{0,2},{2,4},{4,6},{6,8},{8,10},{10,12},{12,14},{14,16},{16,18},{18... | collective-permute-start | bytes 3145736 | tf_op jit(solution)/shard_map/ppermute | solution.py:15
  102.3 1.5 pad_maximum_fusion.1
  103.8 9.4 %collective-permute-done.6 = bf16[256,2048]{1,0:T(8,128)(2,1)S(1)} collective-permute-done((bf16[256,2048]{1,0:T(8,128)(2,1)S(1)}, bf16[256,2048]{1,0:T(8,128)(2,1)S(1)}, u32[]{:S(2)}, u32[]{:S(2)}) %collective-permute-start.6) | collective-permute-done | bytes 1048608 | tf_op jit(solution)/shard_map/ppermute | solution.py:15
  113.2 1.1 fusion.193
  114.3 1.3 copy.190
  115.6 0.4 select_reduce_fusion
  116.2 1.3 fusion.63
  117.5 0.4 select_reduce_fusion.1
  118.1 1.3 fusion.65
  119.4 1.3 copy.185
  120.7 0.4 select_reduce_fusion.3
  121.6 0.4 select_reduce_fusion.2
  122.6 0.6 copy-done.1
  125.4 87.4 %collective-permute-done.1 = f32[16,256]{1,0:T(8,128)S(1)} collective-permute-done((f32[16,256]{1,0:T(8,128)S(1)}, f32[16,256]{1,0:T(8,128)S(1)}, u32[]{:S(2)}, u32[]{:S(2)}) %collective-permute-start.1) | collective-permute-done | bytes 16416 | tf_op jit(solution)/shard_map/ppermute | solution.py:15
  213.1 2.0 collective-permute-start.10
  215.2 4.4 %collective-permute-done.4 = f32[16,256]{1,0:T(8,128)S(1)} collective-permute-done((f32[16,256]{1,0:T(8,128)S(1)}, f32[16,256]{1,0:T(8,128)S(1)}, u32[]{:S(2)}, u32[]{:S(2)}) %collective-permute-start.4) | collective-permute-done | bytes 16416 | tf_op jit(solution)/shard_map/ppermute | solution.py:15
  220.0 7.9 %collective-permute-done.7 = f32[16,256]{1,0:T(8,128)S(1)} collective-permute-done((f32[16,256]{1,0:T(8,128)S(1)}, f32[16,256]{1,0:T(8,128)S(1)}, u32[]{:S(2)}, u32[]{:S(2)}) %collective-permute-start.7) | collective-permute-done | bytes 16416 | tf_op jit(solution)/shard_map/ppermute | solution.py:15
  228.3 3.0 %fusion.6 = bf16[256,2048]{0,1:T(8,128)(2,1)S(1)} fusion(f32[256,2048]{0,1:T(8,128)S(1)} %collective-permute-done.8, f32[256,2048]{0,1:T(8,128)} %collective-permute-done.5, f32[256,2048]{0,1:T(8,128)} %collective-permute-done.2, f32[128,2048]{0,1:T(8,128)S(1)} %copy-done, f32[128,2048]{0,1:T(8,128)S(1)} %fusion.30, f32[256,16]{0,1:T(8,128)S(1)} %get-tuple-element.34, ...), kind=kLoop, calls=%fused_computation.13 | loop fusion | flops 6291456 | bytes 9551872 | tf_op jit(solution)/shard_map/convert_element_type | solution.py:108
  231.3 0.6 copy.199
  232.0 16.7 %all_to_all.70 = bf16[2,128,2048]{2,1,0:T(8,128)(2,1)S(1)} all-to-all(bf16[2,128,2048]{2,1,0:T(8,128)(2,1)S(1)} %bitcast.431), channel_id=1, replica_groups=mesh['ctx'=128,'head'=2] {'head'}, dimensions={0} | all-to-all | bytes 2097152 | tf_op jit(solution)/shard_map/all_to_all | solution.py:110
  248.7 0.7 copy.200
  249.4 1.3 copy.201
  (106 shorter events, 11.7 us)
Async XLA Ops:
  0.0 18.6 %copy-start.7 = (bf16[128,4096]{1,0:T(8,128)(2,1)S(1)}, bf16[128,4096]{1,0:T(8,128)(2,1)}, u32[]{:S(2)}) copy-start(bf16[128,4096]{1,0:T(8,128)(2,1)} %param.4) | copy-start | bytes 3145732
  1.9 11.9 %all-to-all-start = ((bf16[128,2,512]{0,2,1:T(8,128)(2,1)}), bf16[128,2,512]{0,2,1:T(8,128)(2,1)S(1)}, u32[]{:S(2)}, u32[]{:S(2)}) async-start(bf16[128,2,512]{0,2,1:T(8,128)(2,1)} %bitcast.1), calls=%async_computation | async-start | bytes 524288 | tf_op jit(solution)/shard_map/all_to_all | solution.py:83
  13.8 9.7 %all-to-all-start.2 = ((bf16[128,2,512]{0,2,1:T(8,128)(2,1)}), bf16[128,2,512]{0,2,1:T(8,128)(2,1)S(1)}, u32[]{:S(2)}, u32[]{:S(2)}) async-start(bf16[128,2,512]{0,2,1:T(8,128)(2,1)} %bitcast.9), calls=%async_computation.2 | async-start | bytes 524288 | tf_op jit(solution)/shard_map/all_to_all | solution.py:84
  23.5 16.2 %all-to-all-start.1 = ((bf16[128,2,2048]{0,2,1:T(8,128)(2,1)}), bf16[128,2,2048]{0,2,1:T(8,128)(2,1)S(1)}, u32[]{:S(2)}, u32[]{:S(2)}) async-start(bf16[128,2,2048]{0,2,1:T(8,128)(2,1)} %bitcast.5), calls=%async_computation.1 | async-start | bytes 2097152 | tf_op jit(solution)/shard_map/all_to_all | solution.py:82
  42.9 13.1 %collective-permute-start = (bf16[256,2048]{1,0:T(8,128)(2,1)}, bf16[256,2048]{1,0:T(8,128)(2,1)S(1)}, u32[]{:S(2)}, u32[]{:S(2)}) collective-permute-start(bf16[256,2048]{1,0:T(8,128)(2,1)} %bitcast.52), channel_id=1, source_target_pairs={{0,2},{2,4},{4,6},{6,8},{8,10},{10,12},{12,14},{14,16},{16,18},{18... | collective-permute-start | bytes 3145736 | tf_op jit(solution)/shard_map/ppermute | solution.py:15
  56.0 1.3 copy-start.8
  64.2 1.2 copy-start.3
  64.2 1.5 copy-start.5
  64.8 1.4 copy-start.9
  66.2 18.3 %collective-permute-start.3 = (bf16[256,2048]{1,0:T(8,128)(2,1)S(1)}, bf16[256,2048]{1,0:T(8,128)(2,1)S(1)}, u32[]{:S(2)}, u32[]{:S(2)}) collective-permute-start(bf16[256,2048]{1,0:T(8,128)(2,1)S(1)} %copy-done.9), channel_id=1, source_target_pairs={{0,2},{2,4},{4,6},{6,8},{8,10},{10,12},{12,14},{14,16},{16,18},{18... | collective-permute-start | bytes 3145736 | tf_op jit(solution)/shard_map/ppermute | solution.py:15
  75.1 153.2 %collective-permute-start.2 = (f32[256,2048]{0,1:T(8,128)}, f32[256,2048]{0,1:T(8,128)}, u32[]{:S(2)}, u32[]{:S(2)}) collective-permute-start(f32[256,2048]{0,1:T(8,128)} %pad_maximum_fusion), channel_id=1, source_target_pairs={{0,254},{2,0},{4,2},{6,4},{8,6},{10,8},{12,10},{14,12},{16,14},{18... | collective-permute-start | bytes 6291464 | tf_op jit(solution)/shard_map/ppermute | solution.py:15
  84.6 1.3 copy-start.10
  92.7 1.2 copy-start.4
  92.8 1.5 copy-start.6
  93.3 1.4 copy-start.11
  94.8 18.4 %collective-permute-start.6 = (bf16[256,2048]{1,0:T(8,128)(2,1)S(1)}, bf16[256,2048]{1,0:T(8,128)(2,1)S(1)}, u32[]{:S(2)}, u32[]{:S(2)}) collective-permute-start(bf16[256,2048]{1,0:T(8,128)(2,1)S(1)} %copy-done.11), channel_id=1, source_target_pairs={{0,2},{2,4},{4,6},{6,8},{8,10},{10,12},{12,14},{14,16},{16,18},{18... | collective-permute-start | bytes 3145736 | tf_op jit(solution)/shard_map/ppermute | solution.py:15
  103.8 124.5 %collective-permute-start.5 = (f32[256,2048]{0,1:T(8,128)}, f32[256,2048]{0,1:T(8,128)}, u32[]{:S(2)}, u32[]{:S(2)}) collective-permute-start(f32[256,2048]{0,1:T(8,128)} %pad_maximum_fusion.1), channel_id=1, source_target_pairs={{0,252},{2,254},{4,0},{6,2},{8,4},{10,6},{12,8},{14,10},{16,12},{1... | collective-permute-start | bytes 6291464 | tf_op jit(solution)/shard_map/ppermute | solution.py:15
  122.0 1.2 copy-start.1
  122.0 1.5 copy-start.2
  123.9 104.4 %collective-permute-start.8 = (f32[256,2048]{0,1:T(8,128)S(1)}, f32[256,2048]{0,1:T(8,128)S(1)}, u32[]{:S(2)}, u32[]{:S(2)}) collective-permute-start(f32[256,2048]{0,1:T(8,128)S(1)} %pad_maximum_fusion.2), channel_id=1, source_target_pairs={{0,250},{2,252},{4,254},{6,0},{8,2},{10,4},{12,6},{14,8},{16,10},{... | collective-permute-start | bytes 6291464 | tf_op jit(solution)/shard_map/ppermute | solution.py:15
  124.7 103.5 %copy-start = (f32[128,2048]{0,1:T(8,128)S(1)}, f32[128,2048]{0,1:T(8,128)}, u32[]{:S(2)}) copy-start(f32[128,2048]{0,1:T(8,128)} %fusion.29) | copy-start | bytes 3145732
  124.9 87.8 %collective-permute-start.1 = (f32[16,256]{1,0:T(8,128)S(1)}, f32[16,256]{1,0:T(8,128)S(1)}, u32[]{:S(2)}, u32[]{:S(2)}) collective-permute-start(f32[16,256]{1,0:T(8,128)S(1)} %pad_maximum_fusion.4), channel_id=1, source_target_pairs={{0,254},{2,0},{4,2},{6,4},{8,6},{10,8},{12,10},{14,12},{16,14},{18... | collective-permute-start | bytes 49160 | tf_op jit(solution)/shard_map/ppermute | solution.py:15
  125.3 87.9 %collective-permute-start.9 = (f32[16,256]{1,0:T(8,128)S(1)}, f32[16,256]{1,0:T(8,128)S(1)}, u32[]{:S(2)}, u32[]{:S(2)}) collective-permute-start(f32[16,256]{1,0:T(8,128)S(1)} %pad_maximum_fusion.7), channel_id=1, source_target_pairs={{0,254},{2,0},{4,2},{6,4},{8,6},{10,8},{12,10},{14,12},{16,14},{18... | collective-permute-start | bytes 49160 | tf_op jit(solution)/shard_map/ppermute | solution.py:15
  212.8 6.8 %collective-permute-start.4 = (f32[16,256]{1,0:T(8,128)S(1)}, f32[16,256]{1,0:T(8,128)S(1)}, u32[]{:S(2)}, u32[]{:S(2)}) collective-permute-start(f32[16,256]{1,0:T(8,128)S(1)} %pad_maximum_fusion.5), channel_id=1, source_target_pairs={{0,252},{2,254},{4,0},{6,2},{8,4},{10,6},{12,8},{14,10},{16,12},{1... | collective-permute-start | bytes 49160 | tf_op jit(solution)/shard_map/ppermute | solution.py:15
  213.1 6.8 %collective-permute-start.10 = (f32[16,256]{1,0:T(8,128)S(1)}, f32[16,256]{1,0:T(8,128)S(1)}, u32[]{:S(2)}, u32[]{:S(2)}) collective-permute-start(f32[16,256]{1,0:T(8,128)S(1)} %pad_maximum_fusion.8), channel_id=1, source_target_pairs={{0,252},{2,254},{4,0},{6,2},{8,4},{10,6},{12,8},{14,10},{16,12},{1... | collective-permute-start | bytes 49160 | tf_op jit(solution)/shard_map/ppermute | solution.py:15
  219.6 8.3 %collective-permute-start.7 = (f32[16,256]{1,0:T(8,128)S(1)}, f32[16,256]{1,0:T(8,128)S(1)}, u32[]{:S(2)}, u32[]{:S(2)}) collective-permute-start(f32[16,256]{1,0:T(8,128)S(1)} %pad_maximum_fusion.6), channel_id=1, source_target_pairs={{0,250},{2,252},{4,254},{6,0},{8,2},{10,4},{12,6},{14,8},{16,10},{... | collective-permute-start | bytes 49160 | tf_op jit(solution)/shard_map/ppermute | solution.py:15
  219.9 8.3 %collective-permute-start.11 = (f32[16,256]{1,0:T(8,128)S(1)}, f32[16,256]{1,0:T(8,128)S(1)}, u32[]{:S(2)}, u32[]{:S(2)}) collective-permute-start(f32[16,256]{1,0:T(8,128)S(1)} %pad_maximum_fusion.9), channel_id=1, source_target_pairs={{0,250},{2,252},{4,254},{6,0},{8,2},{10,4},{12,6},{14,8},{16,10},{... | collective-permute-start | bytes 49160 | tf_op jit(solution)/shard_map/ppermute | solution.py:15
where the time goes:
time: 254 us; the launch traced here: 251 us
  waiting for transfers between devices  145 us (57%)
  starting transfers between devices  28 us (11%)
  local copies, waits for them, and re-layouts  25.8 us (10%)
  matrix products  17.3 us (7%)
  blocking collectives  16.7 us (7%)
  other arithmetic  11.9 us (5%)
  between operations  5.65 us (2%)
    ppermute x12, waiting for transfers between devices, from_behind(): lax.ppermute(array, axis, [(i, (i + by) % devices) for i in range(devices)])  129 us
    ppermute x12, starting transfers between devices, from_behind(): lax.ppermute(array, axis, [(i, (i + by) % devices) for i in range(devices)])  16.8 us
    all_to_all x1, blocking collectives, shards(): lax.all_to_all(attention, 'head', split_axis=0, concat_axis=1, tiled=True)  16.7 us
    all_to_all x1, waiting for transfers between devices, shards(): lax.all_to_all(queries, 'head', split_axis=1, concat_axis=0, tiled=True)  12.3 us
    dot_general x16, matrix products, tile_part(): jnp.einsum('grab,bgd->agrd', rounded, v_three, preferred_element_type=jnp...  11.4 us
    slice x10, local copies, waits for them, and re-layouts, block_part(): q_block[first * half:(first + 1) * half]  11.4 us
    unnamed x26, local copies, waits for them, and re-layouts  6.44 us
    dot_general x16, matrix products, tile_part(): jnp.einsum('agrd,bgd->grab', q_four, k_three, preferred_element_type=jnp....  5.93 us
  transfers between devices with their start and end apart: 15, of which 11 were waited for; matrix products, arithmetic and copies ran while one was open for 13% of the time, Pallas kernels for 0%

commit v1 on v0

v1 whole, which is shorter than its diff:
```python
import jax
import jax.numpy as jnp
from jax import lax
from jax.experimental import pallas as pl
from jax.experimental.pallas import tpu as pltpu
from jax.sharding import PartitionSpec as P

HEAD_DIM = 128
KV_HEADS = 8
SHARE = 4
ROWS = 128
AXES = ("ctx", "head")
SCALE = HEAD_DIM**-0.5
LOG2E = 1.4426950408889634
HIDDEN = 1e30


def pairs_from(cycle, source):
    pairs = []
    for c in range(cycle):
        for h in range(2):
            origin = source(c, h)
            if origin is not None:
                pairs.append((origin[0] % cycle * 2 + origin[1], c * 2 + h))
    return pairs


def send(array, pairs):
    return lax.ppermute(array, AXES, pairs)


def attend(flags, q_ref, keys, values, out_ref):
    count = len(keys)
    ones = jnp.ones((ROWS * count, HEAD_DIM), jnp.bfloat16)
    row = lax.broadcasted_iota(jnp.int32, (SHARE * ROWS, ROWS), 0) % ROWS
    col = lax.broadcasted_iota(jnp.int32, (SHARE * ROWS, ROWS), 1)
    below = col <= row

    def group(g, carry):
        kv = pl.ds(pl.multiple_of(g * HEAD_DIM, HEAD_DIM), HEAD_DIM)
        q = jnp.concatenate(
            [
                q_ref[:, pl.ds(pl.multiple_of((g * SHARE + s) * HEAD_DIM, HEAD_DIM), HEAD_DIM)]
                for s in range(SHARE)
            ],
            axis=0,
        )
        scores = []
        top = None
        for j in range(count):
            part = lax.dot_general(
                q, keys[j][:, kv], (((1,), (1,)), ((), ())), preferred_element_type=jnp.float32
            )
            if j == 0:
                part = jnp.where(below, part, -HIDDEN)
                peak = jnp.max(part, axis=1, keepdims=True)
                top = peak
            else:
                peak = jnp.max(part, axis=1, keepdims=True)
                top = jnp.maximum(top, jnp.where(flags[j] > 0, peak, -HIDDEN))
            scores.append(part)
        weights = []
        for j in range(count):
            shift = top if j == 0 else jnp.where(flags[j] > 0, top, HIDDEN)
            weights.append(jnp.exp2((scores[j] - shift) * (SCALE * LOG2E)).astype(jnp.bfloat16))
        weights = jnp.concatenate(weights, axis=1)
        v = jnp.concatenate([values[j][:, kv] for j in range(count)], axis=0)
        both = jnp.dot(
            weights, jnp.concatenate([v, ones], axis=1), preferred_element_type=jnp.float32
        )
        mixed = (both[:, :HEAD_DIM] / both[:, HEAD_DIM:]).astype(jnp.bfloat16)
        for s in range(SHARE):
            out_ref[:, pl.ds(pl.multiple_of((g * SHARE + s) * HEAD_DIM, HEAD_DIM), HEAD_DIM)] = (
                mixed[s * ROWS : (s + 1) * ROWS]
            )
        return carry

    lax.fori_loop(0, KV_HEADS, group, 0)


def whole(flags_ref, q_ref, *refs):
    out_ref, k_pick, v_pick = refs[-3], refs[-2], refs[-1]
    tiles = refs[:-3]
    keys = [tiles[i] for i in range(6)]
    values = [tiles[10 + i] for i in range(6)]
    core = flags_ref[8]

    @pl.when(core == 0)
    def _():
        for n in range(2):
            k_pick[n] = tiles[6 + n][...]
            v_pick[n] = tiles[16 + n][...]

    @pl.when(core != 0)
    def _():
        for n in range(2):
            k_pick[n] = tiles[8 + n][...]
            v_pick[n] = tiles[18 + n][...]

    keys += [k_pick.at[0], k_pick.at[1]]
    values += [v_pick.at[0], v_pick.at[1]]
    flags = [flags_ref[j] for j in range(8)]
    attend(flags, q_ref, keys, values, out_ref)


def shards(queries, keys, values, block_place):
    cycle = lax.axis_size("ctx")
    routes = {
        "pair": pairs_from(cycle, lambda c, h: (c, 1 - h)),
        "next": pairs_from(cycle, lambda c, h: (c + 2, h)),
        "core": pairs_from(cycle, lambda c, h: (c ^ 1, h)),
        "down": pairs_from(cycle, lambda c, h: (c + 1, h) if c % 2 == 0 else None),
        "far": pairs_from(cycle, lambda c, h: (c + 1, h) if c % 2 == 1 else None),
        "cross": pairs_from(cycle, lambda c, h: (c + 1, 1 - h) if c % 2 == 1 else None),
    }

    def spread(a):
        b = send(a, routes["pair"])
        c = send(a, routes["next"])
        d = send(a, routes["down"])
        e = send(b, routes["down"])
        f = send(c, routes["core"])
        g = send(c, routes["pair"])
        far = send(c, routes["far"])
        cross = send(c, routes["cross"])
        j = send(g, routes["core"])
        return [a, b, c, f, g, j, d, e, far, cross]

    c = lax.axis_index("ctx")
    h = lax.axis_index("head")
    core = c % 2
    mate = c + 1 - 2 * core
    blocks = jnp.stack([c, c, c + 2, mate + 2, c + 2, mate + 2, c + 1 + 2 * core, c + 1 + 2 * core])
    halves = jnp.stack([h, 1 - h, h, h, 1 - h, 1 - h, h, 1 - h])
    place = block_place[(blocks % cycle) * 2 + halves]
    own = block_place[2 * c + h]
    flags = jnp.concatenate([(place < own).astype(jnp.int32), core[None].astype(jnp.int32)])
    vmem = pl.BlockSpec(memory_space=pltpu.VMEM)
    return pl.pallas_call(
        whole,
        out_shape=jax.ShapeDtypeStruct(queries.shape, queries.dtype),
        in_specs=[pl.BlockSpec(memory_space=pltpu.SMEM)] + [vmem] * 21,
        out_specs=vmem,
        scratch_shapes=[
            pltpu.VMEM((2, ROWS, KV_HEADS * HEAD_DIM), jnp.bfloat16),
            pltpu.VMEM((2, ROWS, KV_HEADS * HEAD_DIM), jnp.bfloat16),
        ],
        compiler_params=pltpu.CompilerParams(vmem_limit_bytes=40 * 1024 * 1024),
        cost_estimate=pl.CostEstimate(flops=2 * 10**9, bytes_accessed=6 * 2**20, transcendentals=2**22),
    )(flags, queries, *spread(keys), *spread(values))


def solution(mesh):
    spec = P(AXES, None)
    return jax.shard_map(
        shards, mesh=mesh, in_specs=(spec, spec, spec, P()), out_specs=spec, check_vma=False
    )
```

time: 254 us -> 69 us (0.27)
  the two profiles are of different devices: /device:TPU:239 before, /device:TPU:1 now
where the time goes in v1:
time: 69 us; the launch traced here: 68.7 us
  starting transfers between devices  51.6 us (75%)
  Pallas kernels  11.3 us (16%)
  local copies, waits for them, and re-layouts  3.4 us (5%)
  waiting for transfers between devices  1.54 us (2%)
  other arithmetic  0.77 us (1%)
    ppermute x18, starting transfers between devices, send(): return lax.ppermute(array, AXES, pairs)  51.6 us
    pallas_call x1, Pallas kernels, shards(): pl.pallas_call(whole, out_shape=jax.ShapeDtypeStruct(queries.shape, queri...  11.3 us
    unnamed x8, local copies, waits for them, and re-layouts  1.91 us
    ppermute x18, waiting for transfers between devices, send(): return lax.ppermute(array, AXES, pairs)  1.54 us
  transfers between devices with their start and end apart: 18, of which 4 were waited for; matrix products, arithmetic and copies ran while one was open for 3% of the time, Pallas kernels for 0%

profile of v1, /device:TPU:1, one launch (start us, length us, event | category | flops | bytes accessed | tf_op | source)
XLA Modules:
  0.0 68.7 jit_solution(7039830577289612817)
XLA Ops:
  0.0 9.6 %collective-permute-start.1 = (bf16[128,1024]{1,0:T(8,128)(2,1)}, bf16[128,1024]{1,0:T(8,128)(2,1)S(1)}, u32[]{:S(2)}, u32[]{:S(2)}) collective-permute-start(bf16[128,1024]{1,0:T(8,128)(2,1)} %refs_0_.1), channel_id=1, source_target_pairs={{4,0},{5,1},{6,2},{7,3},{8,4},{9,5},{10,6},{11,7},{12,8},{13,9},{1... | collective-permute-start | bytes 786440 | tf_op jit(solution)/shard_map/ppermute | solution.py:29
  9.6 2.6 %collective-permute-start = (bf16[128,1024]{1,0:T(8,128)(2,1)}, bf16[128,1024]{1,0:T(8,128)(2,1)S(1)}, u32[]{:S(2)}, u32[]{:S(2)}) collective-permute-start(bf16[128,1024]{1,0:T(8,128)(2,1)} %refs_0_.1), channel_id=1, source_target_pairs={{1,0},{0,1},{3,2},{2,3},{5,4},{4,5},{7,6},{6,7},{9,8},{8,9},{11,10... | collective-permute-start | bytes 786440 | tf_op jit(solution)/shard_map/ppermute | solution.py:29
  12.2 3.1 %collective-permute-start.5 = (bf16[128,1024]{1,0:T(8,128)(2,1)}, bf16[128,1024]{1,0:T(8,128)(2,1)S(1)}, u32[]{:S(2)}, u32[]{:S(2)}) collective-permute-start(bf16[128,1024]{1,0:T(8,128)(2,1)} %refs_0_.1), channel_id=1, source_target_pairs={{2,0},{3,1},{6,4},{7,5},{10,8},{11,9},{14,12},{15,13},{18,16},{19,... | collective-permute-start | bytes 786440 | tf_op jit(solution)/shard_map/ppermute | solution.py:29
  15.4 0.2 collective-permute-start.10
  15.6 1.6 %collective-permute-start.9 = (bf16[128,1024]{1,0:T(8,128)(2,1)}, bf16[128,1024]{1,0:T(8,128)(2,1)S(1)}, u32[]{:S(2)}, u32[]{:S(2)}) collective-permute-start(bf16[128,1024]{1,0:T(8,128)(2,1)} %refs_10_.1), channel_id=1, source_target_pairs={{1,0},{0,1},{3,2},{2,3},{5,4},{4,5},{7,6},{6,7},{9,8},{8,9},{11,10... | collective-permute-start | bytes 786440 | tf_op jit(solution)/shard_map/ppermute | solution.py:29
  17.1 0.0 collective-permute-done.1.refs_2_
  17.2 1.8 %collective-permute-start.14 = (bf16[128,1024]{1,0:T(8,128)(2,1)}, bf16[128,1024]{1,0:T(8,128)(2,1)S(1)}, u32[]{:S(2)}, u32[]{:S(2)}) collective-permute-start(bf16[128,1024]{1,0:T(8,128)(2,1)} %refs_10_.1), channel_id=1, source_target_pairs={{2,0},{3,1},{6,4},{7,5},{10,8},{11,9},{14,12},{15,13},{18,16},{19,... | collective-permute-start | bytes 786440 | tf_op jit(solution)/shard_map/ppermute | solution.py:29
  19.0 0.0 collective-permute-done.refs_1_
  19.0 1.3 %collective-permute-start.8 = (bf16[128,1024]{1,0:T(8,128)(2,1)S(1)}, bf16[128,1024]{1,0:T(8,128)(2,1)S(1)}, u32[]{:S(2)}, u32[]{:S(2)}) collective-permute-start(bf16[128,1024]{1,0:T(8,128)(2,1)S(1)} %collective-permute-done.1.refs_2_), channel_id=1, source_target_pairs={{5,2},{4,3},{9,6},{8,7},{13,10},{12,11},{17,14},{16,15},{21,18},{2... | collective-permute-start | bytes 786440 | tf_op jit(solution)/shard_map/ppermute | solution.py:29
  20.3 0.0 collective-permute-done.5.refs_6_
  20.3 1.3 %collective-permute-start.7 = (bf16[128,1024]{1,0:T(8,128)(2,1)S(1)}, bf16[128,1024]{1,0:T(8,128)(2,1)S(1)}, u32[]{:S(2)}, u32[]{:S(2)}) collective-permute-start(bf16[128,1024]{1,0:T(8,128)(2,1)S(1)} %collective-permute-done.1.refs_2_), channel_id=1, source_target_pairs={{4,2},{5,3},{8,6},{9,7},{12,10},{13,11},{16,14},{17,15},{20,18},{2... | collective-permute-start | bytes 786440 | tf_op jit(solution)/shard_map/ppermute | solution.py:29
  21.6 0.0 copy-start.3
  21.6 0.7 copy-done.3
  22.3 0.6 dynamic_slice.3
  23.0 0.1 stack.41
  23.1 0.1 stack.38
  23.2 0.7 collective-permute-done.10.refs_12_
  23.8 2.0 %collective-permute-start.3 = (bf16[128,1024]{1,0:T(8,128)(2,1)S(1)}, bf16[128,1024]{1,0:T(8,128)(2,1)S(1)}, u32[]{:S(2)}, u32[]{:S(2)}) collective-permute-start(bf16[128,1024]{1,0:T(8,128)(2,1)S(1)} %collective-permute-done.1.refs_2_), channel_id=1, source_target_pairs={{1,0},{0,1},{3,2},{2,3},{5,4},{4,5},{7,6},{6,7},{9,8},{8,9},{11,10... | collective-permute-start | bytes 786440 | tf_op jit(solution)/shard_map/ppermute | solution.py:29
  25.9 0.0 collective-permute-done.9.refs_11_
  25.9 12.4 %collective-permute-start.2 = (bf16[128,1024]{1,0:T(8,128)(2,1)S(1)}, bf16[128,1024]{1,0:T(8,128)(2,1)S(1)}, u32[]{:S(2)}, u32[]{:S(2)}) collective-permute-start(bf16[128,1024]{1,0:T(8,128)(2,1)S(1)} %collective-permute-done.1.refs_2_), channel_id=1, source_target_pairs={{2,0},{3,1},{0,2},{1,3},{6,4},{7,5},{4,6},{5,7},{10,8},{11,9},{8,1... | collective-permute-start | bytes 786440 | tf_op jit(solution)/shard_map/ppermute | solution.py:29
  38.3 0.0 collective-permute-done.14.refs_16_
  38.3 1.3 %collective-permute-start.17 = (bf16[128,1024]{1,0:T(8,128)(2,1)S(1)}, bf16[128,1024]{1,0:T(8,128)(2,1)S(1)}, u32[]{:S(2)}, u32[]{:S(2)}) collective-permute-start(bf16[128,1024]{1,0:T(8,128)(2,1)S(1)} %collective-permute-done.10.refs_12_), channel_id=1, source_target_pairs={{5,2},{4,3},{9,6},{8,7},{13,10},{12,11},{17,14},{16,15},{21,18},{2... | collective-permute-start | bytes 786440 | tf_op jit(solution)/shard_map/ppermute | solution.py:29
  39.6 0.0 collective-permute-done.8.refs_9_
  39.6 1.9 %collective-permute-start.12 = (bf16[128,1024]{1,0:T(8,128)(2,1)S(1)}, bf16[128,1024]{1,0:T(8,128)(2,1)}, u32[]{:S(2)}, u32[]{:S(2)}) collective-permute-start(bf16[128,1024]{1,0:T(8,128)(2,1)S(1)} %collective-permute-done.10.refs_12_), channel_id=1, source_target_pairs={{1,0},{0,1},{3,2},{2,3},{5,4},{4,5},{7,6},{6,7},{9,8},{8,9},{11,10... | collective-permute-start | bytes 786440 | tf_op jit(solution)/shard_map/ppermute | solution.py:29
  41.5 0.0 collective-permute-done.7.refs_8_
  41.5 5.6 %collective-permute-start.6 = (bf16[128,1024]{1,0:T(8,128)(2,1)S(1)}, bf16[128,1024]{1,0:T(8,128)(2,1)}, u32[]{:S(2)}, u32[]{:S(2)}) collective-permute-start(bf16[128,1024]{1,0:T(8,128)(2,1)S(1)} %collective-permute-done.refs_1_), channel_id=1, source_target_pairs={{2,0},{3,1},{6,4},{7,5},{10,8},{11,9},{14,12},{15,13},{18,16},{19,... | collective-permute-start | bytes 786440 | tf_op jit(solution)/shard_map/ppermute | solution.py:29
  47.1 0.0 copy-start.1
  47.2 0.0 copy-start.2
  47.2 0.6 gather_fusion
  47.8 0.0 collective-permute-done.3.refs_4_
  47.8 1.3 %collective-permute-start.16 = (bf16[128,1024]{1,0:T(8,128)(2,1)S(1)}, bf16[128,1024]{1,0:T(8,128)(2,1)S(1)}, u32[]{:S(2)}, u32[]{:S(2)}) collective-permute-start(bf16[128,1024]{1,0:T(8,128)(2,1)S(1)} %collective-permute-done.10.refs_12_), channel_id=1, source_target_pairs={{4,2},{5,3},{8,6},{9,7},{12,10},{13,11},{16,14},{17,15},{20,18},{2... | collective-permute-start | bytes 786440 | tf_op jit(solution)/shard_map/ppermute | solution.py:29
  49.1 0.0 collective-permute-done.2.refs_3_
  49.1 2.9 %collective-permute-start.11 = (bf16[128,1024]{1,0:T(8,128)(2,1)S(1)}, bf16[128,1024]{1,0:T(8,128)(2,1)S(1)}, u32[]{:S(2)}, u32[]{:S(2)}) collective-permute-start(bf16[128,1024]{1,0:T(8,128)(2,1)S(1)} %collective-permute-done.10.refs_12_), channel_id=1, source_target_pairs={{2,0},{3,1},{0,2},{1,3},{6,4},{7,5},{4,6},{5,7},{10,8},{11,9},{8,1... | collective-permute-start | bytes 786440 | tf_op jit(solution)/shard_map/ppermute | solution.py:29
  52.1 0.0 collective-permute-done.6.refs_7_
  52.1 1.9 %collective-permute-start.15 = (bf16[128,1024]{1,0:T(8,128)(2,1)S(1)}, bf16[128,1024]{1,0:T(8,128)(2,1)S(1)}, u32[]{:S(2)}, u32[]{:S(2)}) collective-permute-start(bf16[128,1024]{1,0:T(8,128)(2,1)S(1)} %collective-permute-done.9.refs_11_), channel_id=1, source_target_pairs={{2,0},{3,1},{6,4},{7,5},{10,8},{11,9},{14,12},{15,13},{18,16},{19,... | collective-permute-start | bytes 786440 | tf_op jit(solution)/shard_map/ppermute | solution.py:29
  54.0 0.0 collective-permute-done.17.refs_19_
  54.0 0.1 collective-permute-start.4
  54.1 0.0 collective-permute-done.12.refs_14_
  54.1 0.5 collective-permute-start.13
  54.6 0.7 compare_convert_fusion
  55.3 0.1 pad_add_fusion.flags_ref
  55.4 0.1 collective-permute-done.16.refs_18_
  55.5 0.0 collective-permute-done.11.refs_13_
  55.5 0.0 collective-permute-done.15.refs_17_
  55.5 0.1 collective-permute-done.4.refs_5_
  55.7 0.6 collective-permute-done.13.refs_15_
  56.2 0.0 copy-done.1
  56.2 0.0 copy-done.2
  56.2 0.0 copy-start
  56.3 1.2 %copy-done = bf16[128,4096]{1,0:T(8,128)(2,1)S(1)} copy-done((bf16[128,4096]{1,0:T(8,128)(2,1)S(1)}, bf16[128,4096]{1,0:T(8,128)(2,1)}, u32[]{:S(2)}) %copy-start) | copy-done | bytes 1048600
  57.5 11.3 %shard_map.46 = bf16[128,4096]{1,0:T(8,128)(2,1)} custom-call(s32[9]{0:T(128)S(1)} %pad_add_fusion.flags_ref, bf16[128,4096]{1,0:T(8,128)(2,1)S(1)} %copy-done, bf16[128,1024]{1,0:T(8,128)(2,1)S(1)} %copy-done.1, bf16[128,1024]{1,0:T(8,128)(2,1)S(1)} %collective-permute-done.refs_1_, bf16[128,1024]{1,0:T(8,128)(2,1)S(1)} %collective-permute-done.1.refs_2_, ...), custom_call_target="tpu_custom_call" | custom-call | flops 2000000000 | bytes 6291456 | tf_op jit(solution)/shard_map/pallas_call | solution.py:139
  (2 shorter events, 0.0 us)
Async XLA Ops:
  0.0 17.1 %collective-permute-start.1 = (bf16[128,1024]{1,0:T(8,128)(2,1)}, bf16[128,1024]{1,0:T(8,128)(2,1)S(1)}, u32[]{:S(2)}, u32[]{:S(2)}) collective-permute-start(bf16[128,1024]{1,0:T(8,128)(2,1)} %refs_0_.1), channel_id=1, source_target_pairs={{4,0},{5,1},{6,2},{7,3},{8,4},{9,5},{10,6},{11,7},{12,8},{13,9},{1... | collective-permute-start | bytes 786440 | tf_op jit(solution)/shard_map/ppermute | solution.py:29
  9.6 9.4 %collective-permute-start = (bf16[128,1024]{1,0:T(8,128)(2,1)}, bf16[128,1024]{1,0:T(8,128)(2,1)S(1)}, u32[]{:S(2)}, u32[]{:S(2)}) collective-permute-start(bf16[128,1024]{1,0:T(8,128)(2,1)} %refs_0_.1), channel_id=1, source_target_pairs={{1,0},{0,1},{3,2},{2,3},{5,4},{4,5},{7,6},{6,7},{9,8},{8,9},{11,10... | collective-permute-start | bytes 786440 | tf_op jit(solution)/shard_map/ppermute | solution.py:29
  12.2 8.1 %collective-permute-start.5 = (bf16[128,1024]{1,0:T(8,128)(2,1)}, bf16[128,1024]{1,0:T(8,128)(2,1)S(1)}, u32[]{:S(2)}, u32[]{:S(2)}) collective-permute-start(bf16[128,1024]{1,0:T(8,128)(2,1)} %refs_0_.1), channel_id=1, source_target_pairs={{2,0},{3,1},{6,4},{7,5},{10,8},{11,9},{14,12},{15,13},{18,16},{19,... | collective-permute-start | bytes 786440 | tf_op jit(solution)/shard_map/ppermute | solution.py:29
  15.4 8.4 %collective-permute-start.10 = (bf16[128,1024]{1,0:T(8,128)(2,1)}, bf16[128,1024]{1,0:T(8,128)(2,1)S(1)}, u32[]{:S(2)}, u32[]{:S(2)}) collective-permute-start(bf16[128,1024]{1,0:T(8,128)(2,1)} %refs_10_.1), channel_id=1, source_target_pairs={{4,0},{5,1},{6,2},{7,3},{8,4},{9,5},{10,6},{11,7},{12,8},{13,9},{1... | collective-permute-start | bytes 786440 | tf_op jit(solution)/shard_map/ppermute | solution.py:29
  15.6 10.3 %collective-permute-start.9 = (bf16[128,1024]{1,0:T(8,128)(2,1)}, bf16[128,1024]{1,0:T(8,128)(2,1)S(1)}, u32[]{:S(2)}, u32[]{:S(2)}) collective-permute-start(bf16[128,1024]{1,0:T(8,128)(2,1)} %refs_10_.1), channel_id=1, source_target_pairs={{1,0},{0,1},{3,2},{2,3},{5,4},{4,5},{7,6},{6,7},{9,8},{8,9},{11,10... | collective-permute-start | bytes 786440 | tf_op jit(solution)/shard_map/ppermute | solution.py:29
  17.2 21.2 %collective-permute-start.14 = (bf16[128,1024]{1,0:T(8,128)(2,1)}, bf16[128,1024]{1,0:T(8,128)(2,1)S(1)}, u32[]{:S(2)}, u32[]{:S(2)}) collective-permute-start(bf16[128,1024]{1,0:T(8,128)(2,1)} %refs_10_.1), channel_id=1, source_target_pairs={{2,0},{3,1},{6,4},{7,5},{10,8},{11,9},{14,12},{15,13},{18,16},{19,... | collective-permute-start | bytes 786440 | tf_op jit(solution)/shard_map/ppermute | solution.py:29
  19.0 20.6 %collective-permute-start.8 = (bf16[128,1024]{1,0:T(8,128)(2,1)S(1)}, bf16[128,1024]{1,0:T(8,128)(2,1)S(1)}, u32[]{:S(2)}, u32[]{:S(2)}) collective-permute-start(bf16[128,1024]{1,0:T(8,128)(2,1)S(1)} %collective-permute-done.1.refs_2_), channel_id=1, source_target_pairs={{5,2},{4,3},{9,6},{8,7},{13,10},{12,11},{17,14},{16,15},{21,18},{2... | collective-permute-start | bytes 786440 | tf_op jit(solution)/shard_map/ppermute | solution.py:29
  20.3 21.2 %collective-permute-start.7 = (bf16[128,1024]{1,0:T(8,128)(2,1)S(1)}, bf16[128,1024]{1,0:T(8,128)(2,1)S(1)}, u32[]{:S(2)}, u32[]{:S(2)}) collective-permute-start(bf16[128,1024]{1,0:T(8,128)(2,1)S(1)} %collective-permute-done.1.refs_2_), channel_id=1, source_target_pairs={{4,2},{5,3},{8,6},{9,7},{12,10},{13,11},{16,14},{17,15},{20,18},{2... | collective-permute-start | bytes 786440 | tf_op jit(solution)/shard_map/ppermute | solution.py:29
  21.6 0.7 copy-start.3
  23.8 24.0 %collective-permute-start.3 = (bf16[128,1024]{1,0:T(8,128)(2,1)S(1)}, bf16[128,1024]{1,0:T(8,128)(2,1)S(1)}, u32[]{:S(2)}, u32[]{:S(2)}) collective-permute-start(bf16[128,1024]{1,0:T(8,128)(2,1)S(1)} %collective-permute-done.1.refs_2_), channel_id=1, source_target_pairs={{1,0},{0,1},{3,2},{2,3},{5,4},{4,5},{7,6},{6,7},{9,8},{8,9},{11,10... | collective-permute-start | bytes 786440 | tf_op jit(solution)/shard_map/ppermute | solution.py:29
  25.9 23.2 %collective-permute-start.2 = (bf16[128,1024]{1,0:T(8,128)(2,1)S(1)}, bf16[128,1024]{1,0:T(8,128)(2,1)S(1)}, u32[]{:S(2)}, u32[]{:S(2)}) collective-permute-start(bf16[128,1024]{1,0:T(8,128)(2,1)S(1)} %collective-permute-done.1.refs_2_), channel_id=1, source_target_pairs={{2,0},{3,1},{0,2},{1,3},{6,4},{7,5},{4,6},{5,7},{10,8},{11,9},{8,1... | collective-permute-start | bytes 786440 | tf_op jit(solution)/shard_map/ppermute | solution.py:29
  38.3 15.7 %collective-permute-start.17 = (bf16[128,1024]{1,0:T(8,128)(2,1)S(1)}, bf16[128,1024]{1,0:T(8,128)(2,1)S(1)}, u32[]{:S(2)}, u32[]{:S(2)}) collective-permute-start(bf16[128,1024]{1,0:T(8,128)(2,1)S(1)} %collective-permute-done.10.refs_12_), channel_id=1, source_target_pairs={{5,2},{4,3},{9,6},{8,7},{13,10},{12,11},{17,14},{16,15},{21,18},{2... | collective-permute-start | bytes 786440 | tf_op jit(solution)/shard_map/ppermute | solution.py:29
  39.6 14.5 %collective-permute-start.12 = (bf16[128,1024]{1,0:T(8,128)(2,1)S(1)}, bf16[128,1024]{1,0:T(8,128)(2,1)}, u32[]{:S(2)}, u32[]{:S(2)}) collective-permute-start(bf16[128,1024]{1,0:T(8,128)(2,1)S(1)} %collective-permute-done.10.refs_12_), channel_id=1, source_target_pairs={{1,0},{0,1},{3,2},{2,3},{5,4},{4,5},{7,6},{6,7},{9,8},{8,9},{11,10... | collective-permute-start | bytes 786440 | tf_op jit(solution)/shard_map/ppermute | solution.py:29
  41.5 10.6 %collective-permute-start.6 = (bf16[128,1024]{1,0:T(8,128)(2,1)S(1)}, bf16[128,1024]{1,0:T(8,128)(2,1)}, u32[]{:S(2)}, u32[]{:S(2)}) collective-permute-start(bf16[128,1024]{1,0:T(8,128)(2,1)S(1)} %collective-permute-done.refs_1_), channel_id=1, source_target_pairs={{2,0},{3,1},{6,4},{7,5},{10,8},{11,9},{14,12},{15,13},{18,16},{19,... | collective-permute-start | bytes 786440 | tf_op jit(solution)/shard_map/ppermute | solution.py:29
  47.1 9.1 %copy-start.1 = (bf16[128,1024]{1,0:T(8,128)(2,1)S(1)}, bf16[128,1024]{1,0:T(8,128)(2,1)}, u32[]{:S(2)}) copy-start(bf16[128,1024]{1,0:T(8,128)(2,1)} %refs_0_.1) | copy-start | bytes 786436
  47.2 9.1 %copy-start.2 = (bf16[128,1024]{1,0:T(8,128)(2,1)S(1)}, bf16[128,1024]{1,0:T(8,128)(2,1)}, u32[]{:S(2)}) copy-start(bf16[128,1024]{1,0:T(8,128)(2,1)} %refs_10_.1) | copy-start | bytes 786436
  47.8 7.7 %collective-permute-start.16 = (bf16[128,1024]{1,0:T(8,128)(2,1)S(1)}, bf16[128,1024]{1,0:T(8,128)(2,1)S(1)}, u32[]{:S(2)}, u32[]{:S(2)}) collective-permute-start(bf16[128,1024]{1,0:T(8,128)(2,1)S(1)} %collective-permute-done.10.refs_12_), channel_id=1, source_target_pairs={{4,2},{5,3},{8,6},{9,7},{12,10},{13,11},{16,14},{17,15},{20,18},{2... | collective-permute-start | bytes 786440 | tf_op jit(solution)/shard_map/ppermute | solution.py:29
  49.1 6.4 %collective-permute-start.11 = (bf16[128,1024]{1,0:T(8,128)(2,1)S(1)}, bf16[128,1024]{1,0:T(8,128)(2,1)S(1)}, u32[]{:S(2)}, u32[]{:S(2)}) collective-permute-start(bf16[128,1024]{1,0:T(8,128)(2,1)S(1)} %collective-permute-done.10.refs_12_), channel_id=1, source_target_pairs={{2,0},{3,1},{0,2},{1,3},{6,4},{7,5},{4,6},{5,7},{10,8},{11,9},{8,1... | collective-permute-start | bytes 786440 | tf_op jit(solution)/shard_map/ppermute | solution.py:29
  52.1 3.4 %collective-permute-start.15 = (bf16[128,1024]{1,0:T(8,128)(2,1)S(1)}, bf16[128,1024]{1,0:T(8,128)(2,1)S(1)}, u32[]{:S(2)}, u32[]{:S(2)}) collective-permute-start(bf16[128,1024]{1,0:T(8,128)(2,1)S(1)} %collective-permute-done.9.refs_11_), channel_id=1, source_target_pairs={{2,0},{3,1},{6,4},{7,5},{10,8},{11,9},{14,12},{15,13},{18,16},{19,... | collective-permute-start | bytes 786440 | tf_op jit(solution)/shard_map/ppermute | solution.py:29
  54.0 1.6 %collective-permute-start.4 = (bf16[128,1024]{1,0:T(8,128)(2,1)S(1)}, bf16[128,1024]{1,0:T(8,128)(2,1)S(1)}, u32[]{:S(2)}, u32[]{:S(2)}) collective-permute-start(bf16[128,1024]{1,0:T(8,128)(2,1)S(1)} %collective-permute-done.3.refs_4_), channel_id=1, source_target_pairs={{2,0},{3,1},{0,2},{1,3},{6,4},{7,5},{4,6},{5,7},{10,8},{11,9},{8,1... | collective-permute-start | bytes 786440 | tf_op jit(solution)/shard_map/ppermute | solution.py:29
  54.1 2.1 %collective-permute-start.13 = (bf16[128,1024]{1,0:T(8,128)(2,1)}, bf16[128,1024]{1,0:T(8,128)(2,1)S(1)}, u32[]{:S(2)}, u32[]{:S(2)}) collective-permute-start(bf16[128,1024]{1,0:T(8,128)(2,1)} %collective-permute-done.12.refs_14_), channel_id=1, source_target_pairs={{2,0},{3,1},{0,2},{1,3},{6,4},{7,5},{4,6},{5,7},{10,8},{11,9},{8,1... | collective-permute-start | bytes 786440 | tf_op jit(solution)/shard_map/ppermute | solution.py:29
  56.2 1.2 %copy-start = (bf16[128,4096]{1,0:T(8,128)(2,1)S(1)}, bf16[128,4096]{1,0:T(8,128)(2,1)}, u32[]{:S(2)}) copy-start(bf16[128,4096]{1,0:T(8,128)(2,1)} %q_ref.1) | copy-start | bytes 3145732

commit v2 on v1

v2 whole, which is shorter than its diff:
```python
import jax
import jax.numpy as jnp
from jax import lax
from jax.experimental import pallas as pl
from jax.experimental.pallas import tpu as pltpu
from jax.sharding import PartitionSpec as P

HEAD_DIM = 128
KV_HEADS = 8
SHARE = 4
ROWS = 128
AXES = ("ctx", "head")
SCALE2 = HEAD_DIM**-0.5 * 1.4426950408889634
HIDDEN = 1e30


def pairs_from(cycle, source):
    pairs = []
    for c in range(cycle):
        for h in range(2):
            origin = source(c, h)
            pairs.append((origin[0] % cycle * 2 + origin[1], c * 2 + h))
    return pairs


def send(array, pairs):
    return lax.ppermute(array, AXES, pairs)


def after(array, *others):
    return lax.optimization_barrier((array, *others))[0]


def lanes(index):
    return pl.ds(pl.multiple_of(index * HEAD_DIM, HEAD_DIM), HEAD_DIM)


def window(q, k, v, flags, own, top):
    parts = lax.dot_general(q, k, (((1,), (1,)), ((), ())), preferred_element_type=jnp.float32)
    parts = [parts[:, j * ROWS : (j + 1) * ROWS] for j in range(len(flags))]
    largest = None
    for j, part in enumerate(parts):
        if j == own:
            row = lax.broadcasted_iota(jnp.int32, part.shape, 0)
            col = lax.broadcasted_iota(jnp.int32, part.shape, 1)
            part = parts[j] = jnp.where(col <= row, part, -HIDDEN)
        else:
            part = part + jnp.where(flags[j], 0.0, -HIDDEN)
        largest = part if largest is None else jnp.maximum(largest, part)
    peak = jnp.broadcast_to(jnp.max(largest, axis=1, keepdims=True), (ROWS, HEAD_DIM))
    peak = peak if top is None else jnp.maximum(peak, top)
    weights = []
    for j, part in enumerate(parts):
        shift = peak if j == own else jnp.where(flags[j], peak, HIDDEN)
        weights.append(jnp.exp2((part - shift) * SCALE2).astype(jnp.bfloat16))
    both = jnp.dot(jnp.concatenate(weights, axis=1), v, preferred_element_type=jnp.float32)
    return both[:, :HEAD_DIM], both[:, HEAD_DIM:], peak


def with_ones(values):
    v = jnp.concatenate(values, axis=0)
    return jnp.concatenate([v, jnp.ones_like(v)], axis=1)


def merge(k_hbm, v_hbm, out_ref, sems):
    copies = [
        pltpu.make_async_copy(k_hbm, out_ref.at[:ROWS], sems.at[0]),
        pltpu.make_async_copy(v_hbm, out_ref.at[ROWS:], sems.at[1]),
    ]
    for copy in copies:
        copy.start()
    for copy in copies:
        copy.wait()


def visible(place_ref, slots):
    cycle = lax.axis_size("ctx")
    x = lax.axis_index("ctx")
    y = lax.axis_index("head")
    odd = x & 1
    closing = jnp.where((x & (cycle // 2 - 1)) >= cycle // 2 - 2, 1, 0)
    mine = y ^ (closing & odd)
    theirs = y ^ (closing & (1 - odd))
    mate = x + 1 - 2 * odd
    far = x + 1 + 2 * odd
    table = dict(
        a=(x, y), b=(x, 1 - y), c=(x + 2, mine), f=(mate + 2, theirs),
        g=(x + 2, 1 - mine), j=(mate + 2, 1 - theirs), d=(far, y), e=(far, 1 - y),
    )
    own = place_ref[2 * x + y]
    return [place_ref[2 * (table[s][0] & (cycle - 1)) + table[s][1]] < own for s in slots]


def early(place_ref, q_ref, a, b, c, f, out_ref, sum_ref, top_ref):
    tiles = [a, b, c, f]
    flags = visible(place_ref, 'abcf')

    def group(g, carry):
        k = jnp.concatenate([t[:ROWS, lanes(g)] for t in tiles], axis=0)
        v = with_ones([t[ROWS:, lanes(g)] for t in tiles])
        for s in range(SHARE):
            at = lanes(g * SHARE + s)
            out_ref[:, at], sum_ref[:, at], top_ref[:, at] = window(q_ref[:, at], k, v, flags, 0, None)
        return carry

    lax.fori_loop(0, KV_HEADS, group, 0, unroll=2)


def late(place_ref, q_ref, g_, j_, d, e, h, i, out1, sum1, top1, out_ref):
    flags = visible(place_ref, 'gjde')
    first = (lax.axis_index('ctx') & 1) == 0

    def group(g, carry):
        at = lanes(g)
        k = [g_[:ROWS, at], j_[:ROWS, at], jnp.where(first, d[:ROWS, at], h[:ROWS, at]), jnp.where(first, e[:ROWS, at], i[:ROWS, at])]
        v = [g_[ROWS:, at], j_[ROWS:, at], jnp.where(first, d[ROWS:, at], h[ROWS:, at]), jnp.where(first, e[ROWS:, at], i[ROWS:, at])]
        k = jnp.concatenate(k, axis=0)
        v = with_ones(v)
        for s in range(SHARE):
            at = lanes(g * SHARE + s)
            out, total, peak = window(q_ref[:, at], k, v, flags, None, top1[:, at])
            keep = jnp.exp2((top1[:, at] - peak) * SCALE2)
            out = out1[:, at] * keep + out
            total = sum1[:, at] * keep + total
            out_ref[:, at] = (out / total).astype(jnp.bfloat16)
        return carry

    lax.fori_loop(0, KV_HEADS, group, 0, unroll=2)


SMEM = pl.BlockSpec(memory_space=pltpu.SMEM)
VMEM = pl.BlockSpec(memory_space=pltpu.VMEM)
PARAMS = pltpu.CompilerParams(vmem_limit_bytes=40 * 2**20)
COST = pl.CostEstimate(flops=2**30, bytes_accessed=3 * 2**20, transcendentals=2**21)


def shards(queries, keys, values, block_place):
    cycle = lax.axis_size("ctx")

    def closing(c):
        return c % (cycle // 2) >= cycle // 2 - 2

    def next_half(c, h):
        return 1 - h if closing(c) and c % 2 == 1 else h

    pair = pairs_from(cycle, lambda c, h: (c, 1 - h))
    ahead = pairs_from(cycle, lambda c, h: (c + 2, next_half(c, h)))
    core = pairs_from(cycle, lambda c, h: (c ^ 1, h))
    one = pairs_from(cycle, lambda c, h: (c + 1, h))
    cross = pairs_from(cycle, lambda c, h: (c + 1, 1 - h) if c % 2 == 1 else (c + 1, h))

    a = pl.pallas_call(
        merge,
        out_shape=pltpu.VMEM((2 * ROWS, keys.shape[1]), keys.dtype),
        in_specs=[pl.BlockSpec(memory_space=pl.ANY)] * 2,
        out_specs=VMEM,
        scratch_shapes=[pltpu.SemaphoreType.DMA((2,))],
    )(keys, values)
    b = send(a, pair)
    c = send(a, ahead)
    f = send(c, core)
    g = send(c, pair)
    h = send(c, one)
    i = send(c, cross)
    d = send(after(a, c), core)
    e = send(after(b, c), core)

    full = pltpu.VMEM(queries.shape, jnp.float32)
    state = pl.pallas_call(
        early,
        out_shape=[full] * 3,
        in_specs=[SMEM] + [VMEM] * 5,
        out_specs=[VMEM] * 3,
        compiler_params=PARAMS,
        cost_estimate=COST,
    )(block_place, queries, a, b, c, f)
    j = send(after(g, *state), core)
    return pl.pallas_call(
        late,
        out_shape=jax.ShapeDtypeStruct(queries.shape, queries.dtype),
        in_specs=[SMEM] + [VMEM] * 10,
        out_specs=VMEM,
        compiler_params=PARAMS,
        cost_estimate=COST,
    )(block_place, queries, g, j, d, e, h, i, *state)


def solution(mesh):
    spec = P(AXES, None)
    return jax.shard_map(
        shards, mesh=mesh, in_specs=(spec, spec, spec, P()), out_specs=spec, check_vma=False
    )
```

time: 69 us -> 55.6 us (0.81)
  the two profiles are of different devices: /device:TPU:1 before, /device:TPU:239 now
where the time goes in v2:
time: 55.6 us; the launch traced here: 55.5 us
  waiting for transfers between devices  31.2 us (56%)
  Pallas kernels  12 us (22%)
  starting transfers between devices  10.4 us (19%)
  local copies, waits for them, and re-layouts  1.9 us (3%)
    ppermute x9, waiting for transfers between devices, send(): return lax.ppermute(array, AXES, pairs)  31.2 us
    ppermute x9, starting transfers between devices, send(): return lax.ppermute(array, AXES, pairs)  10.4 us
    pallas_call x1, Pallas kernels, shards(): pl.pallas_call(late, out_shape=jax.ShapeDtypeStruct(queries.shape, querie...  6.39 us
    pallas_call x1, Pallas kernels, shards(): pl.pallas_call(early, out_shape=[full] * 3, in_specs=[SMEM] + [VMEM] * 5,...  4.58 us
    unnamed x4, local copies, waits for them, and re-layouts  1.9 us
  transfers between devices with their start and end apart: 9, of which 4 were waited for; matrix products, arithmetic and copies ran while one was open for 0% of the time, Pallas kernels for 8%

profile of v2, /device:TPU:239, one launch (start us, length us, event | category | flops | bytes accessed | tf_op | source)
XLA Modules:
  0.0 55.5 jit_solution(10322426441455212881)
XLA Ops:
  0.0 1.0 %shard_map.46.a = bf16[256,1024]{1,0:T(8,128)(2,1)S(1)} custom-call(bf16[128,1024]{1,0:T(8,128)(2,1)} %k_hbm.1, bf16[128,1024]{1,0:T(8,128)(2,1)} %v_hbm.1), custom_call_target="tpu_custom_call" | custom-call | tf_op jit(solution)/shard_map/pallas_call | solution.py:152
  1.1 0.8 %collective-permute-start = (bf16[256,1024]{1,0:T(8,128)(2,1)S(1)}, bf16[256,1024]{1,0:T(8,128)(2,1)S(1)}, u32[]{:S(2)}, u32[]{:S(2)}) collective-permute-start(bf16[256,1024]{1,0:T(8,128)(2,1)S(1)} %shard_map.46.a), channel_id=1, source_target_pairs={{4,0},{5,1},{6,2},{7,3},{8,4},{9,5},{10,6},{11,7},{12,8},{13,9},{1... | collective-permute-start | bytes 1572872 | tf_op jit(solution)/shard_map/ppermute | solution.py:27
  1.9 2.0 %collective-permute-start.2 = (bf16[256,1024]{1,0:T(8,128)(2,1)S(1)}, bf16[256,1024]{1,0:T(8,128)(2,1)S(1)}, u32[]{:S(2)}, u32[]{:S(2)}) collective-permute-start(bf16[256,1024]{1,0:T(8,128)(2,1)S(1)} %shard_map.46.a), channel_id=1, source_target_pairs={{1,0},{0,1},{3,2},{2,3},{5,4},{4,5},{7,6},{6,7},{9,8},{8,9},{11,10... | collective-permute-start | bytes 1572872 | tf_op jit(solution)/shard_map/ppermute | solution.py:27
  3.9 14.2 %collective-permute-done.c = bf16[256,1024]{1,0:T(8,128)(2,1)S(1)} collective-permute-done((bf16[256,1024]{1,0:T(8,128)(2,1)S(1)}, bf16[256,1024]{1,0:T(8,128)(2,1)S(1)}, u32[]{:S(2)}, u32[]{:S(2)}) %collective-permute-start) | collective-permute-done | bytes 524320 | tf_op jit(solution)/shard_map/ppermute | solution.py:27
  18.0 2.5 %collective-permute-start.3 = (bf16[256,1024]{1,0:T(8,128)(2,1)S(1)}, bf16[256,1024]{1,0:T(8,128)(2,1)S(1)}, u32[]{:S(2)}, u32[]{:S(2)}) collective-permute-start(bf16[256,1024]{1,0:T(8,128)(2,1)S(1)} %collective-permute-done.c), channel_id=1, source_target_pairs={{2,0},{3,1},{0,2},{1,3},{6,4},{7,5},{4,6},{5,7},{10,8},{11,9},{8,1... | collective-permute-start | bytes 1572872 | tf_op jit(solution)/shard_map/ppermute | solution.py:27
  20.5 1.6 %collective-permute-start.1 = (bf16[256,1024]{1,0:T(8,128)(2,1)S(1)}, bf16[256,1024]{1,0:T(8,128)(2,1)S(1)}, u32[]{:S(2)}, u32[]{:S(2)}) collective-permute-start(bf16[256,1024]{1,0:T(8,128)(2,1)S(1)} %collective-permute-done.c), channel_id=1, source_target_pairs={{1,0},{0,1},{3,2},{2,3},{5,4},{4,5},{7,6},{6,7},{9,8},{8,9},{11,10... | collective-permute-start | bytes 1572872 | tf_op jit(solution)/shard_map/ppermute | solution.py:27
  22.1 0.4 collective-permute-done.2.b
  22.5 1.9 %collective-permute-start.6 = (bf16[256,1024]{1,0:T(8,128)(2,1)S(1)}, bf16[256,1024]{1,0:T(8,128)(2,1)S(1)}, u32[]{:S(2)}, u32[]{:S(2)}) collective-permute-start(bf16[256,1024]{1,0:T(8,128)(2,1)S(1)} %collective-permute-done.2.b), channel_id=1, source_target_pairs={{2,0},{3,1},{0,2},{1,3},{6,4},{7,5},{4,6},{5,7},{10,8},{11,9},{8,1... | collective-permute-start | bytes 1572872 | tf_op jit(solution)/shard_map/ppermute | solution.py:27
  24.4 0.0 collective-permute-start.5
  24.4 0.5 collective-permute-start.7
  24.9 0.0 collective-permute-done.3.f
  24.9 0.0 collective-permute-start.8
  24.9 0.0 copy-start
  24.9 1.2 %copy-done = bf16[128,4096]{1,0:T(8,128)(2,1)S(1)} copy-done((bf16[128,4096]{1,0:T(8,128)(2,1)S(1)}, bf16[128,4096]{1,0:T(8,128)(2,1)}, u32[]{:S(2)}) %copy-start) | copy-done | bytes 1048600
  26.1 0.0 copy-start.1
  26.1 0.7 %copy-done.1 = s32[256]{0:T(256)S(1)} copy-done((s32[256]{0:T(256)S(1)}, s32[256]{0:T(256)}, u32[]{:S(2)}) %copy-start.1) | copy-done | bytes 1048
  26.8 4.6 %shard_map.47 = (f32[128,4096]{1,0:T(8,128)S(1)}, f32[128,4096]{1,0:T(8,128)S(1)}, f32[128,4096]{1,0:T(8,128)S(1)}) custom-call(s32[256]{0:T(256)S(1)} %copy-done.1, bf16[128,4096]{1,0:T(8,128)(2,1)S(1)} %copy-done, bf16[256,1024]{1,0:T(8,128)(2,1)S(1)} %shard_map.46.a, bf16[256,1024]{1,0:T(8,128)(2,1)S(1)} %collective-permute-done.2.b, ...), custom_call_target="tpu_custom_call" | custom-call | flops 1073741824 | bytes 3145728 | tf_op jit(solution)/shard_map/pallas_call | solution.py:169
  31.4 15.1 %collective-permute-done.1.g_ = bf16[256,1024]{1,0:T(8,128)(2,1)S(1)} collective-permute-done((bf16[256,1024]{1,0:T(8,128)(2,1)S(1)}, bf16[256,1024]{1,0:T(8,128)(2,1)S(1)}, u32[]{:S(2)}, u32[]{:S(2)}) %collective-permute-start.1) | collective-permute-done | bytes 524320 | tf_op jit(solution)/shard_map/ppermute | solution.py:27
  46.5 1.1 %collective-permute-start.4 = (bf16[256,1024]{1,0:T(8,128)(2,1)S(1)}, bf16[256,1024]{1,0:T(8,128)(2,1)S(1)}, u32[]{:S(2)}, u32[]{:S(2)}) collective-permute-start(bf16[256,1024]{1,0:T(8,128)(2,1)S(1)} %collective-permute-done.1.g_), channel_id=1, source_target_pairs={{2,0},{3,1},{0,2},{1,3},{6,4},{7,5},{4,6},{5,7},{10,8},{11,9},{8,1... | collective-permute-start | bytes 1572872 | tf_op jit(solution)/shard_map/ppermute | solution.py:27
  47.6 0.0 collective-permute-done.6.e
  47.6 0.0 collective-permute-done.5.d
  47.6 0.0 collective-permute-done.7.h
  47.6 0.0 collective-permute-done.8.i
  47.6 1.5 %collective-permute-done.4.j_ = bf16[256,1024]{1,0:T(8,128)(2,1)S(1)} collective-permute-done((bf16[256,1024]{1,0:T(8,128)(2,1)S(1)}, bf16[256,1024]{1,0:T(8,128)(2,1)S(1)}, u32[]{:S(2)}, u32[]{:S(2)}) %collective-permute-start.4) | collective-permute-done | bytes 524320 | tf_op jit(solution)/shard_map/ppermute | solution.py:27
  49.1 6.4 %shard_map.48 = bf16[128,4096]{1,0:T(8,128)(2,1)} custom-call(s32[256]{0:T(256)S(1)} %copy-done.1, bf16[128,4096]{1,0:T(8,128)(2,1)S(1)} %copy-done, bf16[256,1024]{1,0:T(8,128)(2,1)S(1)} %collective-permute-done.1.g_, bf16[256,1024]{1,0:T(8,128)(2,1)S(1)} %collective-permute-done.4.j_, bf16[256,1024]{1,0:T(8,128)(2,1)S(1)} %collective-permute-done.5.d, ...), custom_call_target="tpu_custom_call" | custom-call | flops 1073741824 | bytes 3145728 | tf_op jit(solution)/shard_map/pallas_call | solution.py:178
Async XLA Ops:
  1.1 17.0 %collective-permute-start = (bf16[256,1024]{1,0:T(8,128)(2,1)S(1)}, bf16[256,1024]{1,0:T(8,128)(2,1)S(1)}, u32[]{:S(2)}, u32[]{:S(2)}) collective-permute-start(bf16[256,1024]{1,0:T(8,128)(2,1)S(1)} %shard_map.46.a), channel_id=1, source_target_pairs={{4,0},{5,1},{6,2},{7,3},{8,4},{9,5},{10,6},{11,7},{12,8},{13,9},{1... | collective-permute-start | bytes 1572872 | tf_op jit(solution)/shard_map/ppermute | solution.py:27
  1.9 20.7 %collective-permute-start.2 = (bf16[256,1024]{1,0:T(8,128)(2,1)S(1)}, bf16[256,1024]{1,0:T(8,128)(2,1)S(1)}, u32[]{:S(2)}, u32[]{:S(2)}) collective-permute-start(bf16[256,1024]{1,0:T(8,128)(2,1)S(1)} %shard_map.46.a), channel_id=1, source_target_pairs={{1,0},{0,1},{3,2},{2,3},{5,4},{4,5},{7,6},{6,7},{9,8},{8,9},{11,10... | collective-permute-start | bytes 1572872 | tf_op jit(solution)/shard_map/ppermute | solution.py:27
  18.0 6.9 %collective-permute-start.3 = (bf16[256,1024]{1,0:T(8,128)(2,1)S(1)}, bf16[256,1024]{1,0:T(8,128)(2,1)S(1)}, u32[]{:S(2)}, u32[]{:S(2)}) collective-permute-start(bf16[256,1024]{1,0:T(8,128)(2,1)S(1)} %collective-permute-done.c), channel_id=1, source_target_pairs={{2,0},{3,1},{0,2},{1,3},{6,4},{7,5},{4,6},{5,7},{10,8},{11,9},{8,1... | collective-permute-start | bytes 1572872 | tf_op jit(solution)/shard_map/ppermute | solution.py:27
  20.5 26.0 %collective-permute-start.1 = (bf16[256,1024]{1,0:T(8,128)(2,1)S(1)}, bf16[256,1024]{1,0:T(8,128)(2,1)S(1)}, u32[]{:S(2)}, u32[]{:S(2)}) collective-permute-start(bf16[256,1024]{1,0:T(8,128)(2,1)S(1)} %collective-permute-done.c), channel_id=1, source_target_pairs={{1,0},{0,1},{3,2},{2,3},{5,4},{4,5},{7,6},{6,7},{9,8},{8,9},{11,10... | collective-permute-start | bytes 1572872 | tf_op jit(solution)/shard_map/ppermute | solution.py:27
  22.5 25.1 %collective-permute-start.6 = (bf16[256,1024]{1,0:T(8,128)(2,1)S(1)}, bf16[256,1024]{1,0:T(8,128)(2,1)S(1)}, u32[]{:S(2)}, u32[]{:S(2)}) collective-permute-start(bf16[256,1024]{1,0:T(8,128)(2,1)S(1)} %collective-permute-done.2.b), channel_id=1, source_target_pairs={{2,0},{3,1},{0,2},{1,3},{6,4},{7,5},{4,6},{5,7},{10,8},{11,9},{8,1... | collective-permute-start | bytes 1572872 | tf_op jit(solution)/shard_map/ppermute | solution.py:27
  24.4 23.2 %collective-permute-start.5 = (bf16[256,1024]{1,0:T(8,128)(2,1)S(1)}, bf16[256,1024]{1,0:T(8,128)(2,1)S(1)}, u32[]{:S(2)}, u32[]{:S(2)}) collective-permute-start(bf16[256,1024]{1,0:T(8,128)(2,1)S(1)} %shard_map.46.a), channel_id=1, source_target_pairs={{2,0},{3,1},{0,2},{1,3},{6,4},{7,5},{4,6},{5,7},{10,8},{11,9},{8,1... | collective-permute-start | bytes 1572872 | tf_op jit(solution)/shard_map/ppermute | solution.py:27
  24.4 23.2 %collective-permute-start.7 = (bf16[256,1024]{1,0:T(8,128)(2,1)S(1)}, bf16[256,1024]{1,0:T(8,128)(2,1)S(1)}, u32[]{:S(2)}, u32[]{:S(2)}) collective-permute-start(bf16[256,1024]{1,0:T(8,128)(2,1)S(1)} %collective-permute-done.c), channel_id=1, source_target_pairs={{2,0},{3,1},{4,2},{5,3},{6,4},{7,5},{8,6},{9,7},{10,8},{11,9},{12,... | collective-permute-start | bytes 1572872 | tf_op jit(solution)/shard_map/ppermute | solution.py:27
  24.9 22.7 %collective-permute-start.8 = (bf16[256,1024]{1,0:T(8,128)(2,1)S(1)}, bf16[256,1024]{1,0:T(8,128)(2,1)S(1)}, u32[]{:S(2)}, u32[]{:S(2)}) collective-permute-start(bf16[256,1024]{1,0:T(8,128)(2,1)S(1)} %collective-permute-done.c), channel_id=1, source_target_pairs={{2,0},{3,1},{5,2},{4,3},{6,4},{7,5},{9,6},{8,7},{10,8},{11,9},{13,... | collective-permute-start | bytes 1572872 | tf_op jit(solution)/shard_map/ppermute | solution.py:27
  24.9 1.2 %copy-start = (bf16[128,4096]{1,0:T(8,128)(2,1)S(1)}, bf16[128,4096]{1,0:T(8,128)(2,1)}, u32[]{:S(2)}) copy-start(bf16[128,4096]{1,0:T(8,128)(2,1)} %q_ref.3) | copy-start | bytes 3145732
  26.1 0.7 %copy-start.1 = (s32[256]{0:T(256)S(1)}, s32[256]{0:T(256)}, u32[]{:S(2)}) copy-start(s32[256]{0:T(256)} %place_ref.3) | copy-start | bytes 3076
  46.5 2.6 %collective-permute-start.4 = (bf16[256,1024]{1,0:T(8,128)(2,1)S(1)}, bf16[256,1024]{1,0:T(8,128)(2,1)S(1)}, u32[]{:S(2)}, u32[]{:S(2)}) collective-permute-start(bf16[256,1024]{1,0:T(8,128)(2,1)S(1)} %collective-permute-done.1.g_), channel_id=1, source_target_pairs={{2,0},{3,1},{0,2},{1,3},{6,4},{7,5},{4,6},{5,7},{10,8},{11,9},{8,1... | collective-permute-start | bytes 1572872 | tf_op jit(solution)/shard_map/ppermute | solution.py:27

commit v3 on v2

--- a/solution.py
+++ b/solution.py
@@ -31,13 +31,24 @@
     return lax.optimization_barrier((array, *others))[0]
 
 
-def lanes(index):
-    return pl.ds(pl.multiple_of(index * HEAD_DIM, HEAD_DIM), HEAD_DIM)
-
-
-def window(q, k, v, flags, own, top):
-    parts = lax.dot_general(q, k, (((1,), (1,)), ((), ())), preferred_element_type=jnp.float32)
-    parts = [parts[:, j * ROWS : (j + 1) * ROWS] for j in range(len(flags))]
+def lanes(first, count=1):
+    return slice(first * HEAD_DIM, (first + count) * HEAD_DIM)
+
+
+def with_ones(values):
+    v = jnp.concatenate(values, axis=0)
+    return jnp.concatenate([v, jnp.ones_like(v)], axis=1)
+
+
+def products(g, q_ref, keys, scores):
+    q = jnp.concatenate([q_ref[:, lanes(g * SHARE + s)] for s in range(SHARE)], axis=0)
+    k = jnp.concatenate(keys, axis=0)
+    scores[g % 2] = lax.dot_general(q, k, (((1,), (1,)), ((), ())), preferred_element_type=jnp.float32)
+
+
+def soften(g, s, scores, weights, flags, own, top):
+    rows = slice(s * ROWS, (s + 1) * ROWS)
+    parts = [scores[g % 2, rows, lanes(j)] for j in range(len(flags))]
     largest = None
     for j, part in enumerate(parts):
         if j == own:
@@ -49,17 +60,20 @@
         largest = part if largest is None else jnp.maximum(largest, part)
     peak = jnp.broadcast_to(jnp.max(largest, axis=1, keepdims=True), (ROWS, HEAD_DIM))
     peak = peak if top is None else jnp.maximum(peak, top)
-    weights = []
     for j, part in enumerate(parts):
         shift = peak if j == own else jnp.where(flags[j], peak, HIDDEN)
-        weights.append(jnp.exp2((part - shift) * SCALE2).astype(jnp.bfloat16))
-    both = jnp.dot(jnp.concatenate(weights, axis=1), v, preferred_element_type=jnp.float32)
-    return both[:, :HEAD_DIM], both[:, HEAD_DIM:], peak
-
-
-def with_ones(values):
-    v = jnp.concatenate(values, axis=0)
-    return jnp.concatenate([v, jnp.ones_like(v)], axis=1)
+        weights[g % 2, rows, lanes(j)] = jnp.exp2((part - shift) * SCALE2).astype(jnp.bfloat16)
+    return peak
+
+
+def staged(first, second, third):
+    for step in range(KV_HEADS + 2):
+        if step >= 2:
+            third(step - 2)
+        if 1 <= step <= KV_HEADS:
+            second(step - 1)
+        if step < KV_HEADS:
+            first(step)
 
 
 def merge(k_hbm, v_hbm, out_ref, sems):
@@ -91,46 +105,103 @@
     return [place_ref[2 * (table[s][0] & (cycle - 1)) + table[s][1]] < own for s in slots]
 
 
-def early(place_ref, q_ref, a, b, c, f, out_ref, sum_ref, top_ref):
-    tiles = [a, b, c, f]
-    flags = visible(place_ref, 'abcf')
-
-    def group(g, carry):
-        k = jnp.concatenate([t[:ROWS, lanes(g)] for t in tiles], axis=0)
+def early(place_ref, q_ref, a, b, out_ref, sum_ref, top_ref, scores, weights):
+    tiles = [a, b]
+    flags = visible(place_ref, "ab")
+
+    def first(g):
+        products(g, q_ref, [t[:ROWS, lanes(g)] for t in tiles], scores)
+
+    def second(g):
+        for s in range(SHARE):
+            top_ref[:, lanes(g * SHARE + s)] = soften(g, s, scores, weights, flags, 0, None)
+
+    def third(g):
         v = with_ones([t[ROWS:, lanes(g)] for t in tiles])
+        both = jnp.dot(weights[g % 2], v, preferred_element_type=jnp.float32)
+        for s in range(SHARE):
+            rows = slice(s * ROWS, (s + 1) * ROWS)
+            out_ref[:, lanes(g * SHARE + s)] = both[rows, :HEAD_DIM]
+            sum_ref[:, lanes(g * SHARE + s)] = both[rows, HEAD_DIM:]
+
+    staged(first, second, third)
+
+
+def middle(place_ref, q_ref, c, f, out1, sum1, top1, out_ref, sum_ref, top_ref, scores, weights, keep):
+    tiles = [c, f]
+    flags = visible(place_ref, "cf")
+
+    def first(g):
+        products(g, q_ref, [t[:ROWS, lanes(g)] for t in tiles], scores)
+
+    def second(g):
         for s in range(SHARE):
             at = lanes(g * SHARE + s)
-            out_ref[:, at], sum_ref[:, at], top_ref[:, at] = window(q_ref[:, at], k, v, flags, 0, None)
-        return carry
-
-    lax.fori_loop(0, KV_HEADS, group, 0, unroll=2)
-
-
-def late(place_ref, q_ref, g_, j_, d, e, h, i, out1, sum1, top1, out_ref):
-    flags = visible(place_ref, 'gjde')
-    first = (lax.axis_index('ctx') & 1) == 0
-
-    def group(g, carry):
-        at = lanes(g)
-        k = [g_[:ROWS, at], j_[:ROWS, at], jnp.where(first, d[:ROWS, at], h[:ROWS, at]), jnp.where(first, e[:ROWS, at], i[:ROWS, at])]
-        v = [g_[ROWS:, at], j_[ROWS:, at], jnp.where(first, d[ROWS:, at], h[ROWS:, at]), jnp.where(first, e[ROWS:, at], i[ROWS:, at])]
-        k = jnp.concatenate(k, axis=0)
-        v = with_ones(v)
+            peak = soften(g, s, scores, weights, flags, None, top1[:, at])
+            keep[g % 2, s * ROWS : (s + 1) * ROWS] = jnp.exp2((top1[:, at] - peak) * SCALE2)
+            top_ref[:, at] = peak
+
+    def third(g):
+        v = with_ones([t[ROWS:, lanes(g)] for t in tiles])
+        both = jnp.dot(weights[g % 2], v, preferred_element_type=jnp.float32)
         for s in range(SHARE):
             at = lanes(g * SHARE + s)
-            out, total, peak = window(q_ref[:, at], k, v, flags, None, top1[:, at])
-            keep = jnp.exp2((top1[:, at] - peak) * SCALE2)
-            out = out1[:, at] * keep + out
-            total = sum1[:, at] * keep + total
+            rows = slice(s * ROWS, (s + 1) * ROWS)
+            factor = keep[g % 2, rows]
+            out_ref[:, at] = out1[:, at] * factor + both[rows, :HEAD_DIM]
+            sum_ref[:, at] = sum1[:, at] * factor + both[rows, HEAD_DIM:]
+
+    staged(first, second, third)
+
+
+def late(place_ref, q_ref, g_, j_, d, e, h, i, out1, sum1, top1, out_hbm, scores, weights, keep, out_ref, sems):
+    flags = visible(place_ref, "gjde")
+    even = (lax.axis_index("ctx") & 1) == 0
+
+    def tiles(rows, at):
+        return [g_[rows, at], j_[rows, at], jnp.where(even, d[rows, at], h[rows, at]), jnp.where(even, e[rows, at], i[rows, at])]
+
+    def leave(g):
+        at = lanes(g * SHARE, SHARE)
+        return pltpu.make_async_copy(out_ref.at[:, at], out_hbm.at[:, at], sems.at[g])
+
+    def first(g):
+        products(g, q_ref, tiles(slice(0, ROWS), lanes(g)), scores)
+
+    def second(g):
+        for s in range(SHARE):
+            top = top1[:, lanes(g * SHARE + s)]
+            peak = soften(g, s, scores, weights, flags, None, top)
+            keep[g % 2, s * ROWS : (s + 1) * ROWS] = jnp.exp2((top - peak) * SCALE2)
+
+    def third(g):
+        v = with_ones(tiles(slice(ROWS, 2 * ROWS), lanes(g)))
+        both = jnp.dot(weights[g % 2], v, preferred_element_type=jnp.float32)
+        for s in range(SHARE):
+            at = lanes(g * SHARE + s)
+            rows = slice(s * ROWS, (s + 1) * ROWS)
+            factor = keep[g % 2, rows]
+            out = out1[:, at] * factor + both[rows, :HEAD_DIM]
+            total = sum1[:, at] * factor + both[rows, HEAD_DIM:]
             out_ref[:, at] = (out / total).astype(jnp.bfloat16)
-        return carry
-
-    lax.fori_loop(0, KV_HEADS, group, 0, unroll=2)
+        leave(g).start()
+
+    staged(first, second, third)
+    for g in range(KV_HEADS):
+        leave(g).wait()
 
 
 SMEM = pl.BlockSpec(memory_space=pltpu.SMEM)
 VMEM = pl.BlockSpec(memory_space=pltpu.VMEM)
-PARAMS = pltpu.CompilerParams(vmem_limit_bytes=40 * 2**20)
+def work(tiles):
+    return [
+        pltpu.VMEM((2, SHARE * ROWS, tiles * ROWS), jnp.float32),
+        pltpu.VMEM((2, SHARE * ROWS, tiles * ROWS), jnp.bfloat16),
+    ]
+
+
+KEEP = pltpu.VMEM((2, SHARE * ROWS, HEAD_DIM), jnp.float32)
+PARAMS = pltpu.CompilerParams(vmem_limit_bytes=16 * 2**20)
 COST = pl.CostEstimate(flops=2**30, bytes_accessed=3 * 2**20, transcendentals=2**21)
 
 
@@ -160,26 +231,43 @@
     c = send(a, ahead)
     f = send(c, core)
     g = send(c, pair)
-    h = send(c, one)
-    i = send(c, cross)
-    d = send(after(a, c), core)
-    e = send(after(b, c), core)
 
     full = pltpu.VMEM(queries.shape, jnp.float32)
     state = pl.pallas_call(
         early,
         out_shape=[full] * 3,
-        in_specs=[SMEM] + [VMEM] * 5,
+        in_specs=[SMEM] + [VMEM] * 3,
         out_specs=[VMEM] * 3,
+        scratch_shapes=work(2),
         compiler_params=PARAMS,
         cost_estimate=COST,
-    )(block_place, queries, a, b, c, f)
+    )(block_place, queries, a, b)
+    c2 = after(c, *state)
+    h = send(c2, one)
+    i = send(c2, cross)
+    state = pl.pallas_call(
+        middle,
+        out_shape=[full] * 3,
+        in_specs=[SMEM] + [VMEM] * 6,
+        out_specs=[VMEM] * 3,
+        scratch_shapes=work(2) + [KEEP],
+        compiler_params=PARAMS,
+        cost_estimate=COST,
+    )(block_place, queries, c, f, *state)
+    d = send(after(a, *state), core)
+    e = send(after(b, *state), core)
     j = send(after(g, *state), core)
     return pl.pallas_call(
         late,
         out_shape=jax.ShapeDtypeStruct(queries.shape, queries.dtype),
         in_specs=[SMEM] + [VMEM] * 10,
-        out_specs=VMEM,
+        out_specs=pl.BlockSpec(memory_space=pl.ANY),
+        scratch_shapes=work(4)
+        + [
+            pltpu.VMEM((2, SHARE * ROWS, HEAD_DIM), jnp.float32),
+            pltpu.VMEM(queries.shape, queries.dtype),
+            pltpu.SemaphoreType.DMA((KV_HEADS,)),
+        ],
         compiler_params=PARAMS,
         cost_estimate=COST,
     )(block_place, queries, g, j, d, e, h, i, *state)

time: 55.6 us -> 53.3 us (0.959); the launches traced: 55.5 us -> 52.6 us
  waiting for transfers between devices: 31.2 us -> 27.1 us
  starting transfers between devices: 10.4 us -> 11.4 us
    ppermute x9, waiting for transfers between devices: 31.2 us -> 27.1 us  [send(): return lax.ppermute(array, AXES, pairs)]
    ppermute x9, starting transfers between devices: 10.4 us -> 11.4 us  [send(): return lax.ppermute(array, AXES, pairs)]
    pallas_call x1, Pallas kernels: 6.39 us -> 5.5 us  [shards(): pl.pallas_call(late, out_shape=jax.ShapeDtypeStruct(queries.shape, querie...]
    pallas_call x1 -> x2, Pallas kernels: 4.58 us -> 5.43 us  [the longest x1 3.18 us: shards(): pl.pallas_call(middle, out_shape=[full] * 3, in_specs=[SMEM] + [VMEM] * 6...]
    unnamed x4 -> x6, local copies, waits for them, and re-layouts: 1.9 us -> 1.91 us
  transfers between devices with their start and end apart: 9 -> 9, of which waited for: 4 -> 4; matrix products, arithmetic and copies ran while one was open for 0% -> 0% of each run, Pallas kernels for 8% -> 10%
where the time goes in v3:
time: 53.3 us; the launch traced here: 52.6 us
  waiting for transfers between devices  27.1 us (51%)
  Pallas kernels  12.1 us (23%)
  starting transfers between devices  11.4 us (21%)
  local copies, waits for them, and re-layouts  1.91 us (4%)
    ppermute x9, waiting for transfers between devices, send(): return lax.ppermute(array, AXES, pairs)  27.1 us
    ppermute x9, starting transfers between devices, send(): return lax.ppermute(array, AXES, pairs)  11.4 us
    pallas_call x1, Pallas kernels, shards(): pl.pallas_call(late, out_shape=jax.ShapeDtypeStruct(queries.shape, querie...  5.5 us
    pallas_call x1, Pallas kernels, shards(): pl.pallas_call(middle, out_shape=[full] * 3, in_specs=[SMEM] + [VMEM] * 6...  3.18 us
    pallas_call x1, Pallas kernels, shards(): pl.pallas_call(early, out_shape=[full] * 3, in_specs=[SMEM] + [VMEM] * 3,...  2.26 us
    unnamed x6, local copies, waits for them, and re-layouts  1.91 us
    pallas_call x1, Pallas kernels, shards(): pl.pallas_call(merge, out_shape=pltpu.VMEM((2 * ROWS, keys.shape[1]), key...  1.13 us
  transfers between devices with their start and end apart: 9, of which 4 were waited for; matrix products, arithmetic and copies ran while one was open for 0% of the time, Pallas kernels for 10%

profile of v3, /device:TPU:239, one launch (start us, length us, event | category | flops | bytes accessed | tf_op | source)
XLA Modules:
  0.0 52.6 jit_solution(290707662328760065)
XLA Ops:
  0.0 0.0 copy-start.1
  0.0 1.1 %shard_map.46.a = bf16[256,1024]{1,0:T(8,128)(2,1)S(1)} custom-call(bf16[128,1024]{1,0:T(8,128)(2,1)} %k_hbm.1, bf16[128,1024]{1,0:T(8,128)(2,1)} %v_hbm.1), custom_call_target="tpu_custom_call" | custom-call | tf_op jit(solution)/shard_map/pallas_call | solution.py:223
  1.1 0.8 %collective-permute-start = (bf16[256,1024]{1,0:T(8,128)(2,1)S(1)}, bf16[256,1024]{1,0:T(8,128)(2,1)S(1)}, u32[]{:S(2)}, u32[]{:S(2)}) collective-permute-start(bf16[256,1024]{1,0:T(8,128)(2,1)S(1)} %shard_map.46.a), channel_id=1, source_target_pairs={{4,0},{5,1},{6,2},{7,3},{8,4},{9,5},{10,6},{11,7},{12,8},{13,9},{1... | collective-permute-start | bytes 1572872 | tf_op jit(solution)/shard_map/ppermute | solution.py:27
  1.9 2.0 %collective-permute-start.3 = (bf16[256,1024]{1,0:T(8,128)(2,1)S(1)}, bf16[256,1024]{1,0:T(8,128)(2,1)S(1)}, u32[]{:S(2)}, u32[]{:S(2)}) collective-permute-start(bf16[256,1024]{1,0:T(8,128)(2,1)S(1)} %shard_map.46.a), channel_id=1, source_target_pairs={{1,0},{0,1},{3,2},{2,3},{5,4},{4,5},{7,6},{6,7},{9,8},{8,9},{11,10... | collective-permute-start | bytes 1572872 | tf_op jit(solution)/shard_map/ppermute | solution.py:27
  4.0 14.2 %collective-permute-done.c = bf16[256,1024]{1,0:T(8,128)(2,1)S(1)} collective-permute-done((bf16[256,1024]{1,0:T(8,128)(2,1)S(1)}, bf16[256,1024]{1,0:T(8,128)(2,1)S(1)}, u32[]{:S(2)}, u32[]{:S(2)}) %collective-permute-start) | collective-permute-done | bytes 524320 | tf_op jit(solution)/shard_map/ppermute | solution.py:27
  18.1 2.5 %collective-permute-start.2 = (bf16[256,1024]{1,0:T(8,128)(2,1)S(1)}, bf16[256,1024]{1,0:T(8,128)(2,1)S(1)}, u32[]{:S(2)}, u32[]{:S(2)}) collective-permute-start(bf16[256,1024]{1,0:T(8,128)(2,1)S(1)} %collective-permute-done.c), channel_id=1, source_target_pairs={{2,0},{3,1},{0,2},{1,3},{6,4},{7,5},{4,6},{5,7},{10,8},{11,9},{8,1... | collective-permute-start | bytes 1572872 | tf_op jit(solution)/shard_map/ppermute | solution.py:27
  20.6 1.6 %collective-permute-start.1 = (bf16[256,1024]{1,0:T(8,128)(2,1)S(1)}, bf16[256,1024]{1,0:T(8,128)(2,1)S(1)}, u32[]{:S(2)}, u32[]{:S(2)}) collective-permute-start(bf16[256,1024]{1,0:T(8,128)(2,1)S(1)} %collective-permute-done.c), channel_id=1, source_target_pairs={{1,0},{0,1},{3,2},{2,3},{5,4},{4,5},{7,6},{6,7},{9,8},{8,9},{11,10... | collective-permute-start | bytes 1572872 | tf_op jit(solution)/shard_map/ppermute | solution.py:27
  22.2 0.4 collective-permute-done.3.b
  22.6 0.0 copy-start
  22.6 1.2 %copy-done = bf16[128,4096]{1,0:T(8,128)(2,1)S(1)} copy-done((bf16[128,4096]{1,0:T(8,128)(2,1)S(1)}, bf16[128,4096]{1,0:T(8,128)(2,1)}, u32[]{:S(2)}) %copy-start) | copy-done | bytes 1048600
  23.8 0.0 copy-start.2
  23.8 0.7 %copy-done.2 = s32[256]{0:T(256)S(1)} copy-done((s32[256]{0:T(256)S(1)}, s32[256]{0:T(256)}, u32[]{:S(2)}) %copy-start.2) | copy-done | bytes 1048
  24.5 2.3 %shard_map.47 = (f32[128,4096]{1,0:T(8,128)S(1)}, f32[128,4096]{1,0:T(8,128)S(1)}, f32[128,4096]{1,0:T(8,128)S(1)}) custom-call(s32[256]{0:T(256)S(1)} %copy-done.2, bf16[128,4096]{1,0:T(8,128)(2,1)S(1)} %copy-done, bf16[256,1024]{1,0:T(8,128)(2,1)S(1)} %shard_map.46.a, bf16[256,1024]{1,0:T(8,128)(2,1)S(1)} %collective-permute-done.3.b), custom_call_target="tpu_custom_call" | custom-call | flops 1073741824 | bytes 3145728 | tf_op jit(solution)/shard_map/pallas_call | solution.py:236
  26.8 1.9 %collective-permute-start.7 = (bf16[256,1024]{1,0:T(8,128)(2,1)S(1)}, bf16[256,1024]{1,0:T(8,128)(2,1)S(1)}, u32[]{:S(2)}, u32[]{:S(2)}) collective-permute-start(bf16[256,1024]{1,0:T(8,128)(2,1)S(1)} %collective-permute-done.c), channel_id=1, source_target_pairs={{2,0},{3,1},{4,2},{5,3},{6,4},{7,5},{8,6},{9,7},{10,8},{11,9},{12,... | collective-permute-start | bytes 1572872 | tf_op jit(solution)/shard_map/ppermute | solution.py:27
  28.7 0.1 collective-permute-start.8
  28.8 0.0 collective-permute-done.2.f
  28.8 0.0 copy-done.1
  28.8 3.2 %shard_map.48 = (f32[128,4096]{1,0:T(8,128)S(1)}, f32[128,4096]{1,0:T(8,128)S(1)}, f32[128,4096]{1,0:T(8,128)S(1)}) custom-call(s32[256]{0:T(256)S(1)} %copy-done.2, bf16[128,4096]{1,0:T(8,128)(2,1)S(1)} %copy-done.1, bf16[256,1024]{1,0:T(8,128)(2,1)S(1)} %collective-permute-done.c, bf16[256,1024]{1,0:T(8,128)(2,1)S(1)} %collective-permute-done.2.f, ...), custom_call_target="tpu_custom_call" | custom-call | flops 1073741824 | bytes 3145728 | tf_op jit(solution)/shard_map/pallas_call | solution.py:248
  32.0 0.1 collective-permute-start.6
  32.1 0.5 collective-permute-start.5
  32.6 10.0 %collective-permute-done.1.g_ = bf16[256,1024]{1,0:T(8,128)(2,1)S(1)} collective-permute-done((bf16[256,1024]{1,0:T(8,128)(2,1)S(1)}, bf16[256,1024]{1,0:T(8,128)(2,1)S(1)}, u32[]{:S(2)}, u32[]{:S(2)}) %collective-permute-start.1) | collective-permute-done | bytes 524320 | tf_op jit(solution)/shard_map/ppermute | solution.py:27
  42.6 1.8 %collective-permute-start.4 = (bf16[256,1024]{1,0:T(8,128)(2,1)S(1)}, bf16[256,1024]{1,0:T(8,128)(2,1)S(1)}, u32[]{:S(2)}, u32[]{:S(2)}) collective-permute-start(bf16[256,1024]{1,0:T(8,128)(2,1)S(1)} %collective-permute-done.1.g_), channel_id=1, source_target_pairs={{2,0},{3,1},{0,2},{1,3},{6,4},{7,5},{4,6},{5,7},{10,8},{11,9},{8,1... | collective-permute-start | bytes 1572872 | tf_op jit(solution)/shard_map/ppermute | solution.py:27
  44.4 0.0 collective-permute-done.7.h
  44.4 2.5 %collective-permute-done.8.i = bf16[256,1024]{1,0:T(8,128)(2,1)S(1)} collective-permute-done((bf16[256,1024]{1,0:T(8,128)(2,1)S(1)}, bf16[256,1024]{1,0:T(8,128)(2,1)S(1)}, u32[]{:S(2)}, u32[]{:S(2)}) %collective-permute-start.8) | collective-permute-done | bytes 524320 | tf_op jit(solution)/shard_map/ppermute | solution.py:27
  46.9 0.0 collective-permute-done.6.e
  46.9 0.0 collective-permute-done.5.d
  46.9 0.0 collective-permute-done.4.j_
  46.9 5.5 %shard_map.49 = bf16[128,4096]{1,0:T(8,128)(2,1)} custom-call(s32[256]{0:T(256)S(1)} %copy-done.2, bf16[128,4096]{1,0:T(8,128)(2,1)S(1)} %copy-done.1, bf16[256,1024]{1,0:T(8,128)(2,1)S(1)} %collective-permute-done.1.g_, bf16[256,1024]{1,0:T(8,128)(2,1)S(1)} %collective-permute-done.4.j_, bf16[256,1024]{1,0:T(8,128)(2,1)S(1)} %collective-permute-done.5.d, ...), custom_call_target="tpu_custom_call" | custom-call | flops 1073741824 | bytes 3145728 | tf_op jit(solution)/shard_map/pallas_call | solution.py:260
Async XLA Ops:
  0.0 28.8 %copy-start.1 = (bf16[128,4096]{1,0:T(8,128)(2,1)S(1)}, bf16[128,4096]{1,0:T(8,128)(2,1)}, u32[]{:S(2)}) copy-start(bf16[128,4096]{1,0:T(8,128)(2,1)} %q_ref.5) | copy-start | bytes 3145732
  1.1 17.0 %collective-permute-start = (bf16[256,1024]{1,0:T(8,128)(2,1)S(1)}, bf16[256,1024]{1,0:T(8,128)(2,1)S(1)}, u32[]{:S(2)}, u32[]{:S(2)}) collective-permute-start(bf16[256,1024]{1,0:T(8,128)(2,1)S(1)} %shard_map.46.a), channel_id=1, source_target_pairs={{4,0},{5,1},{6,2},{7,3},{8,4},{9,5},{10,6},{11,7},{12,8},{13,9},{1... | collective-permute-start | bytes 1572872 | tf_op jit(solution)/shard_map/ppermute | solution.py:27
  1.9 20.7 %collective-permute-start.3 = (bf16[256,1024]{1,0:T(8,128)(2,1)S(1)}, bf16[256,1024]{1,0:T(8,128)(2,1)S(1)}, u32[]{:S(2)}, u32[]{:S(2)}) collective-permute-start(bf16[256,1024]{1,0:T(8,128)(2,1)S(1)} %shard_map.46.a), channel_id=1, source_target_pairs={{1,0},{0,1},{3,2},{2,3},{5,4},{4,5},{7,6},{6,7},{9,8},{8,9},{11,10... | collective-permute-start | bytes 1572872 | tf_op jit(solution)/shard_map/ppermute | solution.py:27
  18.1 10.7 %collective-permute-start.2 = (bf16[256,1024]{1,0:T(8,128)(2,1)S(1)}, bf16[256,1024]{1,0:T(8,128)(2,1)S(1)}, u32[]{:S(2)}, u32[]{:S(2)}) collective-permute-start(bf16[256,1024]{1,0:T(8,128)(2,1)S(1)} %collective-permute-done.c), channel_id=1, source_target_pairs={{2,0},{3,1},{0,2},{1,3},{6,4},{7,5},{4,6},{5,7},{10,8},{11,9},{8,1... | collective-permute-start | bytes 1572872 | tf_op jit(solution)/shard_map/ppermute | solution.py:27
  20.6 22.0 %collective-permute-start.1 = (bf16[256,1024]{1,0:T(8,128)(2,1)S(1)}, bf16[256,1024]{1,0:T(8,128)(2,1)S(1)}, u32[]{:S(2)}, u32[]{:S(2)}) collective-permute-start(bf16[256,1024]{1,0:T(8,128)(2,1)S(1)} %collective-permute-done.c), channel_id=1, source_target_pairs={{1,0},{0,1},{3,2},{2,3},{5,4},{4,5},{7,6},{6,7},{9,8},{8,9},{11,10... | collective-permute-start | bytes 1572872 | tf_op jit(solution)/shard_map/ppermute | solution.py:27
  22.6 1.2 %copy-start = (bf16[128,4096]{1,0:T(8,128)(2,1)S(1)}, bf16[128,4096]{1,0:T(8,128)(2,1)}, u32[]{:S(2)}) copy-start(bf16[128,4096]{1,0:T(8,128)(2,1)} %q_ref.5) | copy-start | bytes 3145732
  23.8 0.7 %copy-start.2 = (s32[256]{0:T(256)S(1)}, s32[256]{0:T(256)}, u32[]{:S(2)}) copy-start(s32[256]{0:T(256)} %place_ref.5) | copy-start | bytes 3076
  26.8 17.6 %collective-permute-start.7 = (bf16[256,1024]{1,0:T(8,128)(2,1)S(1)}, bf16[256,1024]{1,0:T(8,128)(2,1)S(1)}, u32[]{:S(2)}, u32[]{:S(2)}) collective-permute-start(bf16[256,1024]{1,0:T(8,128)(2,1)S(1)} %collective-permute-done.c), channel_id=1, source_target_pairs={{2,0},{3,1},{4,2},{5,3},{6,4},{7,5},{8,6},{9,7},{10,8},{11,9},{12,... | collective-permute-start | bytes 1572872 | tf_op jit(solution)/shard_map/ppermute | solution.py:27
  28.7 18.2 %collective-permute-start.8 = (bf16[256,1024]{1,0:T(8,128)(2,1)S(1)}, bf16[256,1024]{1,0:T(8,128)(2,1)S(1)}, u32[]{:S(2)}, u32[]{:S(2)}) collective-permute-start(bf16[256,1024]{1,0:T(8,128)(2,1)S(1)} %collective-permute-done.c), channel_id=1, source_target_pairs={{2,0},{3,1},{5,2},{4,3},{6,4},{7,5},{9,6},{8,7},{10,8},{11,9},{13,... | collective-permute-start | bytes 1572872 | tf_op jit(solution)/shard_map/ppermute | solution.py:27
  32.0 14.9 %collective-permute-start.6 = (bf16[256,1024]{1,0:T(8,128)(2,1)S(1)}, bf16[256,1024]{1,0:T(8,128)(2,1)S(1)}, u32[]{:S(2)}, u32[]{:S(2)}) collective-permute-start(bf16[256,1024]{1,0:T(8,128)(2,1)S(1)} %collective-permute-done.3.b), channel_id=1, source_target_pairs={{2,0},{3,1},{0,2},{1,3},{6,4},{7,5},{4,6},{5,7},{10,8},{11,9},{8,1... | collective-permute-start | bytes 1572872 | tf_op jit(solution)/shard_map/ppermute | solution.py:27
  32.1 14.8 %collective-permute-start.5 = (bf16[256,1024]{1,0:T(8,128)(2,1)S(1)}, bf16[256,1024]{1,0:T(8,128)(2,1)S(1)}, u32[]{:S(2)}, u32[]{:S(2)}) collective-permute-start(bf16[256,1024]{1,0:T(8,128)(2,1)S(1)} %shard_map.46.a), channel_id=1, source_target_pairs={{2,0},{3,1},{0,2},{1,3},{6,4},{7,5},{4,6},{5,7},{10,8},{11,9},{8,1... | collective-permute-start | bytes 1572872 | tf_op jit(solution)/shard_map/ppermute | solution.py:27
  42.6 4.4 %collective-permute-start.4 = (bf16[256,1024]{1,0:T(8,128)(2,1)S(1)}, bf16[256,1024]{1,0:T(8,128)(2,1)S(1)}, u32[]{:S(2)}, u32[]{:S(2)}) collective-permute-start(bf16[256,1024]{1,0:T(8,128)(2,1)S(1)} %collective-permute-done.1.g_), channel_id=1, source_target_pairs={{2,0},{3,1},{0,2},{1,3},{6,4},{7,5},{4,6},{5,7},{10,8},{11,9},{8,1... | collective-permute-start | bytes 1572872 | tf_op jit(solution)/shard_map/ppermute | solution.py:27

commit v4 on v3

--- a/solution.py
+++ b/solution.py
@@ -77,9 +77,13 @@
 
 
 def merge(k_hbm, v_hbm, out_ref, sems):
+    part = ROWS // 4
     copies = [
-        pltpu.make_async_copy(k_hbm, out_ref.at[:ROWS], sems.at[0]),
-        pltpu.make_async_copy(v_hbm, out_ref.at[ROWS:], sems.at[1]),
+        pltpu.make_async_copy(
+            ref.at[pl.ds(n * part, part)], out_ref.at[pl.ds(base + n * part, part)], sems.at[base // part + n]
+        )
+        for ref, base in ((k_hbm, 0), (v_hbm, ROWS))
+        for n in range(4)
     ]
     for copy in copies:
         copy.start()
@@ -105,9 +109,9 @@
     return [place_ref[2 * (table[s][0] & (cycle - 1)) + table[s][1]] < own for s in slots]
 
 
-def early(place_ref, q_ref, a, b, out_ref, sum_ref, top_ref, scores, weights):
-    tiles = [a, b]
-    flags = visible(place_ref, "ab")
+def early(place_ref, q_ref, a, c, out_ref, sum_ref, top_ref, scores, weights):
+    tiles = [a, c]
+    flags = visible(place_ref, "ac")
 
     def first(g):
         products(g, q_ref, [t[:ROWS, lanes(g)] for t in tiles], scores)
@@ -127,9 +131,9 @@
     staged(first, second, third)
 
 
-def middle(place_ref, q_ref, c, f, out1, sum1, top1, out_ref, sum_ref, top_ref, scores, weights, keep):
-    tiles = [c, f]
-    flags = visible(place_ref, "cf")
+def middle(place_ref, q_ref, b, f, out1, sum1, top1, out_ref, sum_ref, top_ref, scores, weights, keep):
+    tiles = [b, f]
+    flags = visible(place_ref, "bf")
 
     def first(g):
         products(g, q_ref, [t[:ROWS, lanes(g)] for t in tiles], scores)
@@ -154,12 +158,11 @@
     staged(first, second, third)
 
 
-def late(place_ref, q_ref, g_, j_, d, e, h, i, out1, sum1, top1, out_hbm, scores, weights, keep, out_ref, sems):
+def finish(place_ref, q_ref, g_, j_, near, far, out1, sum1, top1, out_hbm, scores, weights, keep, out_ref, sems):
     flags = visible(place_ref, "gjde")
-    even = (lax.axis_index("ctx") & 1) == 0
 
     def tiles(rows, at):
-        return [g_[rows, at], j_[rows, at], jnp.where(even, d[rows, at], h[rows, at]), jnp.where(even, e[rows, at], i[rows, at])]
+        return [t[rows, at] for t in (g_, j_, near, far)]
 
     def leave(g):
         at = lanes(g * SHARE, SHARE)
@@ -191,6 +194,18 @@
         leave(g).wait()
 
 
+def late(place_ref, q_ref, g_, j_, d, e, h, i, *rest):
+    even = (lax.axis_index("ctx") & 1) == 0
+
+    @pl.when(even)
+    def _():
+        finish(place_ref, q_ref, g_, j_, d, e, *rest)
+
+    @pl.when(jnp.logical_not(even))
+    def _():
+        finish(place_ref, q_ref, g_, j_, h, i, *rest)
+
+
 SMEM = pl.BlockSpec(memory_space=pltpu.SMEM)
 VMEM = pl.BlockSpec(memory_space=pltpu.VMEM)
 def work(tiles):
@@ -225,7 +240,7 @@
         out_shape=pltpu.VMEM((2 * ROWS, keys.shape[1]), keys.dtype),
         in_specs=[pl.BlockSpec(memory_space=pl.ANY)] * 2,
         out_specs=VMEM,
-        scratch_shapes=[pltpu.SemaphoreType.DMA((2,))],
+        scratch_shapes=[pltpu.SemaphoreType.DMA((8,))],
     )(keys, values)
     b = send(a, pair)
     c = send(a, ahead)
@@ -241,7 +256,9 @@
         scratch_shapes=work(2),
         compiler_params=PARAMS,
         cost_estimate=COST,
-    )(block_place, queries, a, b)
+    )(block_place, queries, a, c)
+    d = send(after(a, *state), core)
+    e = send(after(b, *state), core)
     c2 = after(c, *state)
     h = send(c2, one)
     i = send(c2, cross)
@@ -253,9 +270,7 @@
         scratch_shapes=work(2) + [KEEP],
         compiler_params=PARAMS,
         cost_estimate=COST,
-    )(block_place, queries, c, f, *state)
-    d = send(after(a, *state), core)
-    e = send(after(b, *state), core)
+    )(block_place, queries, b, f, *state)
     j = send(after(g, *state), core)
     return pl.pallas_call(
         late,

time: 53.3 us -> 53.3 us (level)
  starting transfers between devices: 11.4 us -> 10.1 us
  waiting for transfers between devices: 27.1 us -> 28.4 us
    ppermute x9, waiting for transfers between devices: 27.1 us -> 28.4 us  [send(): return lax.ppermute(array, AXES, pairs)]
    ppermute x9, starting transfers between devices: 11.4 us -> 10.1 us  [send(): return lax.ppermute(array, AXES, pairs)]
  transfers between devices with their start and end apart: 9 -> 9, of which waited for: 4 -> 3; matrix products, arithmetic and copies ran while one was open for 0% -> 0% of each run, Pallas kernels for 10% -> 10%
where the time goes in v4:
time: 53.3 us; the launch traced here: 52.8 us
  waiting for transfers between devices  28.4 us (53%)
  Pallas kernels  12.2 us (23%)
  starting transfers between devices  10.1 us (19%)
  local copies, waits for them, and re-layouts  1.91 us (4%)
    ppermute x9, waiting for transfers between devices, send(): return lax.ppermute(array, AXES, pairs)  28.4 us
    ppermute x9, starting transfers between devices, send(): return lax.ppermute(array, AXES, pairs)  10.1 us
    pallas_call x1, Pallas kernels, shards(): pl.pallas_call(late, out_shape=jax.ShapeDtypeStruct(queries.shape, querie...  5.51 us
    pallas_call x1, Pallas kernels, shards(): pl.pallas_call(middle, out_shape=[full] * 3, in_specs=[SMEM] + [VMEM] * 6...  3.18 us
    pallas_call x1, Pallas kernels, shards(): pl.pallas_call(early, out_shape=[full] * 3, in_specs=[SMEM] + [VMEM] * 3,...  2.27 us
    unnamed x6, local copies, waits for them, and re-layouts  1.91 us
    pallas_call x1, Pallas kernels, shards(): pl.pallas_call(merge, out_shape=pltpu.VMEM((2 * ROWS, keys.shape[1]), key...  1.22 us
  transfers between devices with their start and end apart: 9, of which 3 were waited for; matrix products, arithmetic and copies ran while one was open for 0% of the time, Pallas kernels for 10%

profile of v4, /device:TPU:239, one launch (start us, length us, event | category | flops | bytes accessed | tf_op | source)
XLA Modules:
  0.0 52.8 jit_solution(11260906770238357429)
XLA Ops:
  0.0 0.0 copy-start.1
  0.0 1.2 %shard_map.46.a = bf16[256,1024]{1,0:T(8,128)(2,1)S(1)} custom-call(bf16[128,1024]{1,0:T(8,128)(2,1)} %k_hbm.1, bf16[128,1024]{1,0:T(8,128)(2,1)} %v_hbm.1), custom_call_target="tpu_custom_call" | custom-call | tf_op jit(solution)/shard_map/pallas_call | solution.py:238
  1.2 0.8 %collective-permute-start = (bf16[256,1024]{1,0:T(8,128)(2,1)S(1)}, bf16[256,1024]{1,0:T(8,128)(2,1)S(1)}, u32[]{:S(2)}, u32[]{:S(2)}) collective-permute-start(bf16[256,1024]{1,0:T(8,128)(2,1)S(1)} %shard_map.46.a), channel_id=1, source_target_pairs={{4,0},{5,1},{6,2},{7,3},{8,4},{9,5},{10,6},{11,7},{12,8},{13,9},{1... | collective-permute-start | bytes 1572872 | tf_op jit(solution)/shard_map/ppermute | solution.py:27
  2.0 2.0 %collective-permute-start.2 = (bf16[256,1024]{1,0:T(8,128)(2,1)S(1)}, bf16[256,1024]{1,0:T(8,128)(2,1)S(1)}, u32[]{:S(2)}, u32[]{:S(2)}) collective-permute-start(bf16[256,1024]{1,0:T(8,128)(2,1)S(1)} %shard_map.46.a), channel_id=1, source_target_pairs={{1,0},{0,1},{3,2},{2,3},{5,4},{4,5},{7,6},{6,7},{9,8},{8,9},{11,10... | collective-permute-start | bytes 1572872 | tf_op jit(solution)/shard_map/ppermute | solution.py:27
  4.0 14.2 %collective-permute-done.c = bf16[256,1024]{1,0:T(8,128)(2,1)S(1)} collective-permute-done((bf16[256,1024]{1,0:T(8,128)(2,1)S(1)}, bf16[256,1024]{1,0:T(8,128)(2,1)S(1)}, u32[]{:S(2)}, u32[]{:S(2)}) %collective-permute-start) | collective-permute-done | bytes 524320 | tf_op jit(solution)/shard_map/ppermute | solution.py:27
  18.2 2.5 %collective-permute-start.3 = (bf16[256,1024]{1,0:T(8,128)(2,1)S(1)}, bf16[256,1024]{1,0:T(8,128)(2,1)S(1)}, u32[]{:S(2)}, u32[]{:S(2)}) collective-permute-start(bf16[256,1024]{1,0:T(8,128)(2,1)S(1)} %collective-permute-done.c), channel_id=1, source_target_pairs={{2,0},{3,1},{0,2},{1,3},{6,4},{7,5},{4,6},{5,7},{10,8},{11,9},{8,1... | collective-permute-start | bytes 1572872 | tf_op jit(solution)/shard_map/ppermute | solution.py:27
  20.7 1.6 %collective-permute-start.1 = (bf16[256,1024]{1,0:T(8,128)(2,1)S(1)}, bf16[256,1024]{1,0:T(8,128)(2,1)S(1)}, u32[]{:S(2)}, u32[]{:S(2)}) collective-permute-start(bf16[256,1024]{1,0:T(8,128)(2,1)S(1)} %collective-permute-done.c), channel_id=1, source_target_pairs={{1,0},{0,1},{3,2},{2,3},{5,4},{4,5},{7,6},{6,7},{9,8},{8,9},{11,10... | collective-permute-start | bytes 1572872 | tf_op jit(solution)/shard_map/ppermute | solution.py:27
  22.3 0.0 copy-start
  22.3 1.2 %copy-done = bf16[128,4096]{1,0:T(8,128)(2,1)S(1)} copy-done((bf16[128,4096]{1,0:T(8,128)(2,1)S(1)}, bf16[128,4096]{1,0:T(8,128)(2,1)}, u32[]{:S(2)}) %copy-start) | copy-done | bytes 1048600
  23.5 0.0 copy-start.2
  23.5 0.7 %copy-done.2 = s32[256]{0:T(256)S(1)} copy-done((s32[256]{0:T(256)S(1)}, s32[256]{0:T(256)}, u32[]{:S(2)}) %copy-start.2) | copy-done | bytes 1048
  24.2 2.3 %shard_map.47 = (f32[128,4096]{1,0:T(8,128)S(1)}, f32[128,4096]{1,0:T(8,128)S(1)}, f32[128,4096]{1,0:T(8,128)S(1)}) custom-call(s32[256]{0:T(256)S(1)} %copy-done.2, bf16[128,4096]{1,0:T(8,128)(2,1)S(1)} %copy-done, bf16[256,1024]{1,0:T(8,128)(2,1)S(1)} %shard_map.46.a, bf16[256,1024]{1,0:T(8,128)(2,1)S(1)} %collective-permute-done.c), custom_call_target="tpu_custom_call" | custom-call | flops 1073741824 | bytes 3145728 | tf_op jit(solution)/shard_map/pallas_call | solution.py:251
  26.5 0.9 %collective-permute-start.7 = (bf16[256,1024]{1,0:T(8,128)(2,1)S(1)}, bf16[256,1024]{1,0:T(8,128)(2,1)S(1)}, u32[]{:S(2)}, u32[]{:S(2)}) collective-permute-start(bf16[256,1024]{1,0:T(8,128)(2,1)S(1)} %collective-permute-done.c), channel_id=1, source_target_pairs={{2,0},{3,1},{4,2},{5,3},{6,4},{7,5},{8,6},{9,7},{10,8},{11,9},{12,... | collective-permute-start | bytes 1572872 | tf_op jit(solution)/shard_map/ppermute | solution.py:27
  27.3 0.1 collective-permute-start.8
  27.4 0.0 collective-permute-done.2.b
  27.4 0.1 collective-permute-start.5
  27.5 0.0 collective-permute-done.3.f
  27.5 0.4 collective-permute-start.6
  27.9 0.0 copy-done.1
  27.9 3.2 %shard_map.48 = (f32[128,4096]{1,0:T(8,128)S(1)}, f32[128,4096]{1,0:T(8,128)S(1)}, f32[128,4096]{1,0:T(8,128)S(1)}) custom-call(s32[256]{0:T(256)S(1)} %copy-done.2, bf16[128,4096]{1,0:T(8,128)(2,1)S(1)} %copy-done.1, bf16[256,1024]{1,0:T(8,128)(2,1)S(1)} %collective-permute-done.2.b, bf16[256,1024]{1,0:T(8,128)(2,1)S(1)} %collective-permute-done.3.f, ...), custom_call_target="tpu_custom_call" | custom-call | flops 1073741824 | bytes 3145728 | tf_op jit(solution)/shard_map/pallas_call | solution.py:265
  31.1 11.9 %collective-permute-done.1.g_ = bf16[256,1024]{1,0:T(8,128)(2,1)S(1)} collective-permute-done((bf16[256,1024]{1,0:T(8,128)(2,1)S(1)}, bf16[256,1024]{1,0:T(8,128)(2,1)S(1)}, u32[]{:S(2)}, u32[]{:S(2)}) %collective-permute-start.1) | collective-permute-done | bytes 524320 | tf_op jit(solution)/shard_map/ppermute | solution.py:27
  43.0 1.7 %collective-permute-start.4 = (bf16[256,1024]{1,0:T(8,128)(2,1)S(1)}, bf16[256,1024]{1,0:T(8,128)(2,1)S(1)}, u32[]{:S(2)}, u32[]{:S(2)}) collective-permute-start(bf16[256,1024]{1,0:T(8,128)(2,1)S(1)} %collective-permute-done.1.g_), channel_id=1, source_target_pairs={{2,0},{3,1},{0,2},{1,3},{6,4},{7,5},{4,6},{5,7},{10,8},{11,9},{8,1... | collective-permute-start | bytes 1572872 | tf_op jit(solution)/shard_map/ppermute | solution.py:27
  44.7 0.0 collective-permute-done.5.d
  44.7 0.0 collective-permute-done.6.e
  44.7 0.0 collective-permute-done.7.h
  44.8 2.3 %collective-permute-done.8.i = bf16[256,1024]{1,0:T(8,128)(2,1)S(1)} collective-permute-done((bf16[256,1024]{1,0:T(8,128)(2,1)S(1)}, bf16[256,1024]{1,0:T(8,128)(2,1)S(1)}, u32[]{:S(2)}, u32[]{:S(2)}) %collective-permute-start.8) | collective-permute-done | bytes 524320 | tf_op jit(solution)/shard_map/ppermute | solution.py:27
  47.1 0.0 collective-permute-done.4.j_
  47.1 5.5 %shard_map.49 = bf16[128,4096]{1,0:T(8,128)(2,1)} custom-call(s32[256]{0:T(256)S(1)} %copy-done.2, bf16[128,4096]{1,0:T(8,128)(2,1)S(1)} %copy-done.1, bf16[256,1024]{1,0:T(8,128)(2,1)S(1)} %collective-permute-done.1.g_, bf16[256,1024]{1,0:T(8,128)(2,1)S(1)} %collective-permute-done.4.j_, bf16[256,1024]{1,0:T(8,128)(2,1)S(1)} %collective-permute-done.5.d, ...), custom_call_target="tpu_custom_call" | custom-call | flops 1073741824 | bytes 3145728 | tf_op jit(solution)/shard_map/pallas_call | solution.py:275
Async XLA Ops:
  0.0 27.9 %copy-start.1 = (bf16[128,4096]{1,0:T(8,128)(2,1)S(1)}, bf16[128,4096]{1,0:T(8,128)(2,1)}, u32[]{:S(2)}) copy-start(bf16[128,4096]{1,0:T(8,128)(2,1)} %q_ref.5) | copy-start | bytes 3145732
  1.2 17.0 %collective-permute-start = (bf16[256,1024]{1,0:T(8,128)(2,1)S(1)}, bf16[256,1024]{1,0:T(8,128)(2,1)S(1)}, u32[]{:S(2)}, u32[]{:S(2)}) collective-permute-start(bf16[256,1024]{1,0:T(8,128)(2,1)S(1)} %shard_map.46.a), channel_id=1, source_target_pairs={{4,0},{5,1},{6,2},{7,3},{8,4},{9,5},{10,6},{11,7},{12,8},{13,9},{1... | collective-permute-start | bytes 1572872 | tf_op jit(solution)/shard_map/ppermute | solution.py:27
  2.0 25.4 %collective-permute-start.2 = (bf16[256,1024]{1,0:T(8,128)(2,1)S(1)}, bf16[256,1024]{1,0:T(8,128)(2,1)S(1)}, u32[]{:S(2)}, u32[]{:S(2)}) collective-permute-start(bf16[256,1024]{1,0:T(8,128)(2,1)S(1)} %shard_map.46.a), channel_id=1, source_target_pairs={{1,0},{0,1},{3,2},{2,3},{5,4},{4,5},{7,6},{6,7},{9,8},{8,9},{11,10... | collective-permute-start | bytes 1572872 | tf_op jit(solution)/shard_map/ppermute | solution.py:27
  18.2 9.3 %collective-permute-start.3 = (bf16[256,1024]{1,0:T(8,128)(2,1)S(1)}, bf16[256,1024]{1,0:T(8,128)(2,1)S(1)}, u32[]{:S(2)}, u32[]{:S(2)}) collective-permute-start(bf16[256,1024]{1,0:T(8,128)(2,1)S(1)} %collective-permute-done.c), channel_id=1, source_target_pairs={{2,0},{3,1},{0,2},{1,3},{6,4},{7,5},{4,6},{5,7},{10,8},{11,9},{8,1... | collective-permute-start | bytes 1572872 | tf_op jit(solution)/shard_map/ppermute | solution.py:27
  20.7 22.4 %collective-permute-start.1 = (bf16[256,1024]{1,0:T(8,128)(2,1)S(1)}, bf16[256,1024]{1,0:T(8,128)(2,1)S(1)}, u32[]{:S(2)}, u32[]{:S(2)}) collective-permute-start(bf16[256,1024]{1,0:T(8,128)(2,1)S(1)} %collective-permute-done.c), channel_id=1, source_target_pairs={{1,0},{0,1},{3,2},{2,3},{5,4},{4,5},{7,6},{6,7},{9,8},{8,9},{11,10... | collective-permute-start | bytes 1572872 | tf_op jit(solution)/shard_map/ppermute | solution.py:27
  22.3 1.2 %copy-start = (bf16[128,4096]{1,0:T(8,128)(2,1)S(1)}, bf16[128,4096]{1,0:T(8,128)(2,1)}, u32[]{:S(2)}) copy-start(bf16[128,4096]{1,0:T(8,128)(2,1)} %q_ref.5) | copy-start | bytes 3145732
  23.5 0.7 %copy-start.2 = (s32[256]{0:T(256)S(1)}, s32[256]{0:T(256)}, u32[]{:S(2)}) copy-start(s32[256]{0:T(256)} %place_ref.5) | copy-start | bytes 3076
  26.5 18.3 %collective-permute-start.7 = (bf16[256,1024]{1,0:T(8,128)(2,1)S(1)}, bf16[256,1024]{1,0:T(8,128)(2,1)S(1)}, u32[]{:S(2)}, u32[]{:S(2)}) collective-permute-start(bf16[256,1024]{1,0:T(8,128)(2,1)S(1)} %collective-permute-done.c), channel_id=1, source_target_pairs={{2,0},{3,1},{4,2},{5,3},{6,4},{7,5},{8,6},{9,7},{10,8},{11,9},{12,... | collective-permute-start | bytes 1572872 | tf_op jit(solution)/shard_map/ppermute | solution.py:27
  27.3 19.8 %collective-permute-start.8 = (bf16[256,1024]{1,0:T(8,128)(2,1)S(1)}, bf16[256,1024]{1,0:T(8,128)(2,1)S(1)}, u32[]{:S(2)}, u32[]{:S(2)}) collective-permute-start(bf16[256,1024]{1,0:T(8,128)(2,1)S(1)} %collective-permute-done.c), channel_id=1, source_target_pairs={{2,0},{3,1},{5,2},{4,3},{6,4},{7,5},{9,6},{8,7},{10,8},{11,9},{13,... | collective-permute-start | bytes 1572872 | tf_op jit(solution)/shard_map/ppermute | solution.py:27
  27.4 17.3 %collective-permute-start.5 = (bf16[256,1024]{1,0:T(8,128)(2,1)S(1)}, bf16[256,1024]{1,0:T(8,128)(2,1)S(1)}, u32[]{:S(2)}, u32[]{:S(2)}) collective-permute-start(bf16[256,1024]{1,0:T(8,128)(2,1)S(1)} %shard_map.46.a), channel_id=1, source_target_pairs={{2,0},{3,1},{0,2},{1,3},{6,4},{7,5},{4,6},{5,7},{10,8},{11,9},{8,1... | collective-permute-start | bytes 1572872 | tf_op jit(solution)/shard_map/ppermute | solution.py:27
  27.5 17.2 %collective-permute-start.6 = (bf16[256,1024]{1,0:T(8,128)(2,1)S(1)}, bf16[256,1024]{1,0:T(8,128)(2,1)S(1)}, u32[]{:S(2)}, u32[]{:S(2)}) collective-permute-start(bf16[256,1024]{1,0:T(8,128)(2,1)S(1)} %collective-permute-done.2.b), channel_id=1, source_target_pairs={{2,0},{3,1},{0,2},{1,3},{6,4},{7,5},{4,6},{5,7},{10,8},{11,9},{8,1... | collective-permute-start | bytes 1572872 | tf_op jit(solution)/shard_map/ppermute | solution.py:27
  43.0 4.0 %collective-permute-start.4 = (bf16[256,1024]{1,0:T(8,128)(2,1)S(1)}, bf16[256,1024]{1,0:T(8,128)(2,1)S(1)}, u32[]{:S(2)}, u32[]{:S(2)}) collective-permute-start(bf16[256,1024]{1,0:T(8,128)(2,1)S(1)} %collective-permute-done.1.g_), channel_id=1, source_target_pairs={{2,0},{3,1},{0,2},{1,3},{6,4},{7,5},{4,6},{5,7},{10,8},{11,9},{8,1... | collective-permute-start | bytes 1572872 | tf_op jit(solution)/shard_map/ppermute | solution.py:27
